TPU v7x, 128 devices: a whole 4x4x4 slice. The times are simulated.
128 devices in a mesh: dp: 16 (over x, y_lo, core), tensor: 8 (over y_hi, z).
Axes of the slice: x: 4, y: 4 (y_hi: 2, y_lo: 2; y = y_hi * 2 + y_lo), z: 4, core: 2. Of those that a mesh axis runs over, the one named last changes fastest.
Arguments:
- hidden_in: bfloat16 [16, 1024, 1536], P('dp', 'tensor'), may hold values from -6 to 6
- grad_out: bfloat16 [16, 1024, 1536], P('dp', 'tensor'), may hold values from -6 to 6
- norm_in: float32 [2, 1536], replicated, may hold values from 0.5 to 1.5
- w_z: bfloat16 [2, 1536, 3072], P(None, None, 'tensor'), may hold values from -0.15625 to 0.15625
- w_x: bfloat16 [2, 1536, 3072], P(None, None, 'tensor'), may hold values from -1.7350552 to 1.7350552
- w_bc: bfloat16 [2, 1536, 256], P(None, None, 'tensor'), may hold values from -0.15625 to 0.15625
- w_dt: bfloat16 [2, 1536, 48], P(None, None, 'tensor'), may hold values from -0.15625 to 0.15625
- conv_x: float32 [2, 4, 3072], P(None, None, 'tensor'), may hold values from -3 to 3
- conv_x_bias: float32 [2, 3072], P(None, 'tensor'), may hold values from -3 to 3
- conv_bc: float32 [2, 4, 256], replicated, may hold values from -3 to 3
- conv_bc_bias: float32 [2, 256], replicated, may hold values from -3 to 3
- dt_bias: float32 [2, 48], P(None, 'tensor'), may hold values from -7 to -2.3
- a_log: float32 [2, 48], P(None, 'tensor'), may hold values from 0 to 2.77
- skip: float32 [2, 48], P(None, 'tensor'), may hold values from 0.5 to 2
- norm_gate: float32 [2, 3072], P(None, 'tensor'), may hold values from 0.5 to 1.5
- w_out: bfloat16 [2, 3072, 1536], P(None, 'tensor'), may hold values from -0.109375 to 0.109375
Outputs:
- hidden_out: float32 [16, 1024, 1536], P('dp', 'tensor')
- grad_in: float32 [16, 1024, 1536], P('dp', 'tensor')
- grad_norm_in: float32 [2, 1536], replicated
- grad_w_z: float32 [2, 1536, 3072], P(None, None, 'tensor')
- grad_w_x: float32 [2, 1536, 3072], P(None, None, 'tensor')
- grad_w_bc: float32 [2, 1536, 256], P(None, None, 'tensor')
- grad_w_dt: float32 [2, 1536, 48], P(None, None, 'tensor')
- grad_conv_x: float32 [2, 4, 3072], P(None, None, 'tensor')
- grad_conv_x_bias: float32 [2, 3072], P(None, 'tensor')
- grad_conv_bc: float32 [2, 4, 256], replicated
- grad_conv_bc_bias: float32 [2, 256], replicated
- grad_dt_bias: float32 [2, 48], P(None, 'tensor')
- grad_a_log: float32 [2, 48], P(None, 'tensor')
- grad_skip: float32 [2, 48], P(None, 'tensor')
- grad_norm_gate: float32 [2, 3072], P(None, 'tensor')
- grad_w_out: float32 [2, 3072, 1536], P(None, 'tensor')
All inputs are finite; a program needn't handle non-finite values.
Results may differ from a plain program's by a relative error of at most 0.025.
Values may be sent and summed in bfloat16 or wider, within the bound.
No kernel may reach another device: no remote copies, remote signals or barrier semaphores. Data moves between devices by JAX's collectives and lax.ppermute only.
A program may use at most 192 MiB of HBM per device.

v0:
```python
import jax
import jax.numpy as jnp
from jax import lax
from jax.sharding import PartitionSpec as P

SPAN = 256


epsilon = 1e-05
highest = lax.Precision.HIGHEST


def causal_conv(values, kernel, offset):
    width = kernel.shape[0]
    padded = jnp.pad(values, ((width - 1, 0), (0, 0)))
    summed = offset[None, :] + jnp.zeros_like(values)
    for kernel_tap in range(width):
        summed = (
            summed + kernel[kernel_tap][None, :] * padded[kernel_tap : kernel_tap + values.shape[0]]
        )
    return summed


def span_scan(carried, block_data):
    x_block, b_block, c_block, step_block, rate_block = block_data
    length = rate_block.shape[0]
    row_ids = lax.broadcasted_iota(jnp.int32, (length, length), 0)
    col_ids = lax.broadcasted_iota(jnp.int32, (length, length), 1)
    tri_mask = row_ids >= col_ids
    cumulative = jnp.dot(tri_mask.astype(jnp.float32), rate_block, precision=highest)
    segment = cumulative[:, None, :] - cumulative[None, :, :]
    mask_three = tri_mask[:, :, None]
    decay_mat = jnp.where(mask_three, jnp.exp(jnp.where(mask_three, segment, 0.0)), 0.0)
    scores = jnp.dot(c_block, b_block.T, precision=highest)
    weights = scores[:, :, None] * decay_mat * step_block[None, :, :]
    y_within = jnp.einsum("tsh,shp->thp", weights, x_block, precision=highest)
    y_carried = (
        jnp.einsum("tn,hpn->thp", c_block, carried, precision=highest)
        * jnp.exp(cumulative)[:, :, None]
    )
    tail_weight = jnp.exp(cumulative[-1][None, :] - cumulative) * step_block
    weighted = tail_weight[:, :, None] * x_block
    new_state = jnp.exp(cumulative[-1])[:, None, None] * carried + jnp.einsum(
        "shp,sn->hpn", weighted, b_block, precision=highest
    )
    return (new_state, y_within + y_carried)


def state_scan(x_heads, b_mat, c_mat, step_size, log_decay):
    seq_len, head_count, head_dim = x_heads.shape
    state_dim = b_mat.shape[1]
    block_count = seq_len // SPAN
    blocks = (
        x_heads.reshape(block_count, SPAN, head_count, head_dim),
        b_mat.reshape(block_count, SPAN, state_dim),
        c_mat.reshape(block_count, SPAN, state_dim),
        step_size.reshape(block_count, SPAN, head_count),
        log_decay.reshape(block_count, SPAN, head_count),
    )
    start_state = jnp.zeros((head_count, head_dim, state_dim), jnp.float32)
    last_state, outputs = lax.scan(jax.checkpoint(span_scan), start_state, blocks)
    return outputs.reshape(seq_len, head_count, head_dim)


def mixer_core(
    x_proj,
    bc_proj,
    dt_proj,
    z_proj,
    conv_kernel,
    conv_offset,
    bc_kernel,
    bc_offset,
    dt_offset,
    decay_log,
    skip_gain,
):
    seq_len = x_proj.shape[0]
    head_count = dt_proj.shape[1]
    x_conv = jax.nn.silu(causal_conv(x_proj, conv_kernel, conv_offset))
    bc_conv = jax.nn.silu(causal_conv(bc_proj, bc_kernel, bc_offset))
    state_width = bc_conv.shape[1] // 2
    b_mat = bc_conv[:, :state_width]
    c_mat = bc_conv[:, state_width:]
    step_size = jax.nn.softplus(dt_proj + dt_offset[None, :])
    log_decay = -jnp.exp(decay_log)[None, :] * step_size
    x_heads = x_conv.reshape(seq_len, head_count, -1)
    y_heads = (
        state_scan(x_heads, b_mat, c_mat, step_size, log_decay) + skip_gain[None, :, None] * x_heads
    )
    return y_heads.reshape(seq_len, -1) * jax.nn.silu(z_proj)


def contract_rows(left_mat, right_mat):
    return lax.dot_general(
        left_mat, right_mat, (((0,), (0,)), ((), ())), preferred_element_type=jnp.float32
    )


def contract_cols(left_mat, right_mat):
    return lax.dot_general(
        left_mat, right_mat, (((1,), (1,)), ((), ())), preferred_element_type=jnp.float32
    )


def reduce_grads(head_part, shared_part):
    head_sum = (
        lax.psum(head_part[0].astype(jnp.bfloat16), "dp").astype(jnp.float32),
        lax.psum(head_part[1].astype(jnp.bfloat16), "dp").astype(jnp.float32),
        lax.psum(head_part[2].astype(jnp.bfloat16), "dp").astype(jnp.float32),
        lax.psum(head_part[3].astype(jnp.bfloat16), "dp").astype(jnp.float32),
        lax.psum(head_part[4].astype(jnp.bfloat16), "dp").astype(jnp.float32),
        lax.psum(head_part[5].astype(jnp.bfloat16), "dp").astype(jnp.float32),
        lax.psum(head_part[6].astype(jnp.bfloat16), "dp").astype(jnp.float32),
        lax.psum(head_part[7].astype(jnp.bfloat16), "dp").astype(jnp.float32),
        lax.psum(head_part[8].astype(jnp.bfloat16), "dp").astype(jnp.float32),
        lax.psum(head_part[9].astype(jnp.bfloat16), "dp").astype(jnp.float32),
        lax.psum(head_part[10].astype(jnp.bfloat16), "dp").astype(jnp.float32),
    )
    shared_sum = lax.psum((shared_part[0], shared_part[1], shared_part[2]), ("dp", "tensor"))
    return (tuple(head_sum), tuple(shared_sum))


def local(
    hidden_in,
    grad_out,
    norm_in,
    w_z,
    w_x,
    w_bc,
    w_dt,
    conv_x,
    conv_x_bias,
    conv_bc,
    conv_bc_bias,
    dt_bias,
    a_log,
    skip,
    norm_gate,
    w_out,
):
    layer_count = w_z.shape[0]
    inner_dev = w_z.shape[2]
    state_dev = w_bc.shape[2]
    inner_all = inner_dev * lax.axis_size("tensor")
    residual = hidden_in[0].astype(jnp.float32)
    grad_start = grad_out[0]
    kept_layers = []
    for layer_id in range(layer_count):
        w_cat = jnp.concatenate(
            [w_z[layer_id], w_x[layer_id], w_bc[layer_id], w_dt[layer_id]], axis=1
        )
        inv_rms = lax.rsqrt(jnp.mean(residual * residual, axis=-1, keepdims=True) + epsilon)
        normed = (residual * inv_rms * norm_in[layer_id][None, :]).astype(jnp.bfloat16)
        gathered = lax.all_gather(normed, "tensor", axis=0, tiled=True)
        projected = jnp.dot(gathered, w_cat, preferred_element_type=jnp.float32)
        z_proj = projected[:, :inner_dev]
        x_proj = projected[:, inner_dev : 2 * inner_dev]
        bc_part = projected[:, 2 * inner_dev : 2 * inner_dev + state_dev].astype(jnp.bfloat16)
        dt_proj = projected[:, 2 * inner_dev + state_dev :]
        bc_full = lax.all_gather(bc_part, "tensor", axis=1, tiled=True).astype(jnp.float32)
        gated_vals, core_back = jax.vjp(
            mixer_core,
            x_proj,
            bc_full,
            dt_proj,
            z_proj,
            conv_x[layer_id],
            conv_x_bias[layer_id],
            conv_bc[layer_id],
            conv_bc_bias[layer_id],
            dt_bias[layer_id],
            a_log[layer_id],
            skip[layer_id],
        )
        squares = lax.psum(jnp.sum(gated_vals * gated_vals, axis=-1), "tensor")
        gate_rms = lax.rsqrt(squares / inner_all + epsilon)[:, None]
        gate_out = (gated_vals * gate_rms * norm_gate[layer_id][None, :]).astype(jnp.bfloat16)
        out_weight = w_out[layer_id]
        mixed_part = lax.psum_scatter(
            jnp.dot(gate_out, out_weight, preferred_element_type=jnp.float32),
            "tensor",
            scatter_dimension=0,
            tiled=True,
        )
        kept_layers.append(
            (residual, inv_rms, gathered, w_cat, core_back, gated_vals, gate_rms, gate_out)
        )
        residual = residual + mixed_part
    grad_res = grad_start.astype(jnp.float32)
    layer_grads = [None] * layer_count
    for layer_id in reversed(range(layer_count)):
        res_in, inv_rms, gathered, w_cat, core_back, gated_vals, gate_rms, gate_out = kept_layers[
            layer_id
        ]
        grad_rows = lax.all_gather(grad_res.astype(jnp.bfloat16), "tensor", axis=0, tiled=True)
        g_w_out = contract_rows(gate_out, grad_rows)
        grad_gate_out = contract_cols(grad_rows, w_out[layer_id])
        g_norm_gate = jnp.sum(grad_gate_out * gated_vals * gate_rms, axis=0)
        grad_hat = grad_gate_out * norm_gate[layer_id][None, :]
        products = lax.psum(jnp.sum(grad_hat * gated_vals, axis=-1), "tensor")
        grad_gated = gate_rms * grad_hat - gated_vals * gate_rms**3 * products[:, None] / inner_all
        (
            g_x_proj,
            g_bc_full,
            g_dt_proj,
            g_z_proj,
            g_conv_x,
            g_conv_x_bias,
            g_conv_bc,
            g_conv_bc_bias,
            g_dt_bias,
            g_a_log,
            g_skip,
        ) = core_back(grad_gated)
        g_bc_part = lax.psum_scatter(
            g_bc_full.astype(jnp.bfloat16), "tensor", scatter_dimension=1, tiled=True
        ).astype(jnp.float32)
        grad_cat = jnp.concatenate([g_z_proj, g_x_proj, g_bc_part, g_dt_proj], axis=1).astype(
            jnp.bfloat16
        )
        g_w_cat = contract_rows(gathered, grad_cat)
        grad_normed = lax.psum_scatter(
            contract_cols(grad_cat, w_cat).astype(jnp.bfloat16),
            "tensor",
            scatter_dimension=0,
            tiled=True,
        ).astype(jnp.float32)
        scaled = grad_normed * norm_in[layer_id][None, :]
        gain_terms = grad_normed * res_in * inv_rms
        g_norm_in = jnp.sum(gain_terms, axis=0)
        grad_res = (
            grad_res
            + inv_rms * scaled
            - res_in
            * inv_rms**3
            * jnp.sum(scaled * res_in, axis=-1, keepdims=True)
            / res_in.shape[1]
        )
        head_part = (
            g_w_cat[:, :inner_dev],
            g_w_cat[:, inner_dev : 2 * inner_dev],
            g_w_cat[:, 2 * inner_dev : 2 * inner_dev + state_dev],
            g_w_cat[:, 2 * inner_dev + state_dev :],
            g_conv_x,
            g_conv_x_bias,
            g_dt_bias,
            g_a_log,
            g_skip,
            g_norm_gate,
            g_w_out,
        )
        shared_part = (g_norm_in, g_conv_bc, g_conv_bc_bias)
        layer_grads[layer_id] = (head_part, shared_part)
    head_stack = tuple(
        (
            jnp.stack([layer_grads[layer_id][0][member] for layer_id in range(layer_count)])
            for member in range(11)
        )
    )
    shared_stack = tuple(
        (
            jnp.stack([layer_grads[layer_id][1][member] for layer_id in range(layer_count)])
            for member in range(3)
        )
    )
    head_stack, shared_stack = reduce_grads(head_stack, shared_stack)
    return (
        residual[None],
        grad_res[None],
        shared_stack[0],
        head_stack[0],
        head_stack[1],
        head_stack[2],
        head_stack[3],
        head_stack[4],
        head_stack[5],
        shared_stack[1],
        shared_stack[2],
        head_stack[6],
        head_stack[7],
        head_stack[8],
        head_stack[9],
        head_stack[10],
    )


def solution(mesh):
    return jax.shard_map(
        local,
        mesh=mesh,
        in_specs=(
            P("dp", "tensor", None),
            P("dp", "tensor", None),
            P(),
            P(None, None, "tensor"),
            P(None, None, "tensor"),
            P(None, None, "tensor"),
            P(None, None, "tensor"),
            P(None, None, "tensor"),
            P(None, "tensor"),
            P(),
            P(),
            P(None, "tensor"),
            P(None, "tensor"),
            P(None, "tensor"),
            P(None, "tensor"),
            P(None, "tensor", None),
        ),
        out_specs=(
            P("dp", "tensor", None),
            P("dp", "tensor", None),
            P(),
            P(None, None, "tensor"),
            P(None, None, "tensor"),
            P(None, None, "tensor"),
            P(None, None, "tensor"),
            P(None, None, "tensor"),
            P(None, "tensor"),
            P(),
            P(),
            P(None, "tensor"),
            P(None, "tensor"),
            P(None, "tensor"),
            P(None, "tensor"),
            P(None, "tensor", None),
        ),
        check_vma=False,
    )
```

profile of v0, /device:TPU:1, one launch (start us, length us, event | category | flops | bytes accessed | tf_op | source)
XLA Modules:
  0.0 1638.1 jit_solution(14531042798272911715)
XLA Ops:
  21.5 56.2 %all-gather.6.cloned.1.call-done = bf16[1024,1536]{1,0:T(8,128)(2,1)} async-done(((bf16[128,1536]{1,0:T(8,128)(2,1)}), bf16[1024,1536]{1,0:T(8,128)(2,1)}) %all-gather.6.cloned.1.call-update) | async-done | bytes 3145744 | tf_op jit(solution)/shard_map/all_gather | solution.py:155
  77.7 4.7 fusion.282
  82.6 29.2 %all_gather.19 = bf16[1024,256]{0,1:T(8,128)(2,1)S(1)} all-gather(bf16[1024,32]{0,1:T(8,128)(2,1)S(1)} %slice.567), channel_id=1, replica_groups=mesh['dp'=16,'tensor'=8] {'tensor'}, dimensions={1}, use_global_device_ids=true | all-gather | bytes 589824 | tf_op jit(solution)/shard_map/all_gather | solution.py:161
  124.7 71.5 %while.88 = (s32[]{:T(128)}, f32[6,64,128]{2,1,0:T(8,128)S(1)}, f32[4,256,6,64]{1,0,3,2:T(4,128)}, f32[4,6,64,128]{3,2,1,0:T(8,128)S(1)}, f32[4,256,6]{1,2,0:T(8...) while((s32[]{:T(128)}, f32[6,64,128]{2,1,0:T(8,128)S(1)}, ...), condition=%wide.region_2.4_spmd.clone.clone, body=%wide.region_1.3_spmd.clone.clone.sunk | while | flops 712002560 | bytes 5721377 | solution.py:61
  131.5 9.5 dynamic_update_slice.171
  149.4 9.5 dynamic_update_slice.171
  167.2 9.5 dynamic_update_slice.171
  185.1 9.5 dynamic_update_slice.171
  201.3 16.1 psum.126
  218.0 5.8 fusion.246
  223.9 106.9 %reduce-scatter.7.cloned.1.call-done = f32[128,1536]{1,0:T(8,128)} async-done(((f32[1024,1536]{1,0:T(8,128)}), f32[128,1536]{1,0:T(8,128)}) %reduce-scatter.7.cloned.1.call-update) | async-done | bytes 786448 | tf_op jit(solution)/shard_map/reduce_scatter | solution.py:180
  338.6 56.7 %all-gather.8.cloned.1.call-done = bf16[1024,1536]{1,0:T(8,128)(2,1)} async-done(((bf16[128,1536]{1,0:T(8,128)(2,1)}), bf16[1024,1536]{1,0:T(8,128)(2,1)}) %all-gather.8.cloned.1.call-update) | async-done | bytes 3145744 | tf_op jit(solution)/shard_map/all_gather | solution.py:155
  395.3 5.2 fusion.281
  409.5 30.3 %all_gather.21 = bf16[1024,256]{0,1:T(8,128)(2,1)S(1)} all-gather(bf16[1024,32]{0,1:T(8,128)(2,1)S(1)} %copy-done.73), channel_id=1, replica_groups=mesh['dp'=16,'tensor'=8] {'tensor'}, dimensions={1}, use_global_device_ids=true | all-gather | bytes 589824 | tf_op jit(solution)/shard_map/all_gather | solution.py:161
  448.5 71.6 %while.89 = (s32[]{:T(128)}, f32[6,64,128]{2,1,0:T(8,128)S(1)}, f32[4,256,6,64]{1,0,3,2:T(4,128)}, f32[4,6,64,128]{3,2,1,0:T(8,128)S(1)}, f32[4,256,6]{1,2,0:T(8...) while((s32[]{:T(128)}, f32[6,64,128]{2,1,0:T(8,128)S(1)}, ...), condition=%wide.region_8.10_spmd.clone.clone, body=%wide.region_7.9_spmd.clone.clone.sunk | while | flops 712002560 | bytes 5721377 | solution.py:61
  455.3 9.5 dynamic_update_slice.173
  473.2 9.5 dynamic_update_slice.173
  491.1 9.5 dynamic_update_slice.173
  509.0 9.5 dynamic_update_slice.173
  527.0 15.5 psum.127
  542.5 6.0 multiply_reduce_fusion.6
  548.5 16.9 %psum.128 = f32[1024]{0:T(1024)S(1)} all-reduce(f32[1024]{0:T(1024)S(1)} %get-tuple-element.1315), channel_id=1, replica_groups=mesh['dp'=16,'tensor'=8] {'tensor'}, use_global_device_ids=true, to_apply=%region_13.15 | all-reduce | flops 1024 | bytes 8192 | tf_op jit(solution)/shard_map/psum | solution.py:201
  565.4 6.4 multiply_reduce_fusion.8
  579.2 153.0 %while.86 = (s32[]{:T(128)}, f32[6,64,128]{2,1,0:T(8,128)S(1)}, f32[4,256,6,64]{1,0,3,2:T(4,128)}, f32[4,256,128]{2,1,0:T(8,128)}, f32[4,256,128]{2,1,0:T(8,128)...) while((s32[]{:T(128)}, f32[6,64,128]{2,1,0:T(8,128)S(1)}, ...), condition=%wide.region_23.25_spmd.clone, body=%wide.region_14.24_spmd.clone.sunk | while | flops 1679589888 | bytes 17471092 | solution.py:61
  607.2 9.5 dynamic_update_slice.164
  645.4 9.5 dynamic_update_slice.164
  683.5 9.5 dynamic_update_slice.164
  721.7 9.5 dynamic_update_slice.164
  744.8 6.5 multiply_reduce_fusion.12
  755.7 70.4 %reduce-scatter.11.cloned.1.call-done = bf16[1024,32]{0,1:T(8,128)(2,1)} async-done(((bf16[1024,256]{0,1:T(8,128)(2,1)}), bf16[1024,32]{0,1:T(8,128)(2,1)}) %reduce-scatter.11.cloned.1.call-update) | async-done | bytes 65552 | tf_op jit(solution)/shard_map/reduce_scatter | solution.py:216
  826.1 7.0 convolution_convert_fusion.1
  833.2 79.2 %reduce-scatter.13.cloned.1.call-done = bf16[128,1536]{1,0:T(8,128)(2,1)} async-done(((bf16[1024,1536]{1,0:T(8,128)(2,1)}), bf16[128,1536]{1,0:T(8,128)(2,1)}) %reduce-scatter.13.cloned.1.call-update) | async-done | bytes 393232 | tf_op jit(solution)/shard_map/reduce_scatter | solution.py:223
  916.6 62.2 %all-gather.10.cloned.1.call-done = bf16[1024,1536]{1,0:T(8,128)(2,1)} async-done(((bf16[128,1536]{1,0:T(8,128)(2,1)}), bf16[1024,1536]{1,0:T(8,128)(2,1)}) %all-gather.10.cloned.1.call-update) | async-done | bytes 3145744 | tf_op jit(solution)/shard_map/all_gather | solution.py:196
  978.8 5.9 multiply_reduce_fusion.7
  984.7 15.9 psum.129
  1000.6 5.9 multiply_reduce_fusion.9
  1013.6 154.5 %while.87 = (s32[]{:T(128)}, f32[6,64,128]{2,1,0:T(8,128)S(1)}, f32[4,256,6,64]{1,0,3,2:T(4,128)}, f32[4,256,128]{2,1,0:T(8,128)}, f32[4,256,128]{2,1,0:T(8,128)...) while((s32[]{:T(128)}, f32[6,64,128]{2,1,0:T(8,128)S(1)}, ...), condition=%wide.region_38.40_spmd.clone, body=%wide.region_29.39_spmd.clone.sunk | while | flops 1679589888 | bytes 17176104 | solution.py:61
  1042.2 9.5 dynamic_update_slice.169
  1080.8 9.5 dynamic_update_slice.169
  1119.3 9.5 dynamic_update_slice.169
  1157.9 9.5 dynamic_update_slice.169
  1188.2 63.5 %reduce-scatter.15.cloned.1.call-done = bf16[1024,32]{0,1:T(8,128)(2,1)} async-done(((bf16[1024,256]{0,1:T(8,128)(2,1)}), bf16[1024,32]{0,1:T(8,128)(2,1)}) %reduce-scatter.15.cloned.1.call-update) | async-done | bytes 65552 | tf_op jit(solution)/shard_map/reduce_scatter | solution.py:216
  1251.7 6.6 convolution_convert_fusion
  1259.7 5.8 fusion.242
  1290.1 52.0 %all-reduce.45 = (bf16[2,1536,6]{1,2,0:T(8,128)(2,1)S(1)}, bf16[2,4,384]{2,1,0:T(4,128)(2,1)S(1)}, bf16[2,384]{1,0:T(2,128)(2,1)S(1)}, bf16[2,6]{1,0:T(2,128)(2,...) all-reduce(bf16[2,1536,6]{1,2,0:T(8,128)(2,1)S(1)} %pad_maximum_fus, ...), channel_id=1, replica_groups=mesh['dp'=16,'tensor'=8] {'dp'}, use_global_device_ids=true, to_apply=%region_48.50 | all-reduce | flops 23076 | bytes 92304 | tf_op jit(solution)/shard_map/psum | solution.py:111
  1347.5 77.9 %all-reduce.44 = (f32[2,1536]{1,0:T(2,128)}, f32[2,4,256]{2,1,0:T(4,128)}, f32[2,256]{1,0:T(2,128)}) all-reduce(f32[2,1536]{1,0:T(2,128)S(1)} %pad_maximum_fusion.17, f32[2,4,256]{2,1,0:T(4,128)S(1)} %pad_maximum_fusion.18, f32[2,256]{1,0:T(2,128)S(1)} %pad_maximum_fusion.20), channel_id=1, replica_groups=mesh['dp'=16,'tensor'=8] {'dp','tensor'}, use_global_device_ids=true, to_apply=%region_44.46 | all-reduce | flops 5632 | bytes 45056 | tf_op jit(solution)/shard_map/psum | solution.py:120
  1425.4 15.1 reduce-scatter.9.cloned.1.call-done
  1443.4 175.0 %all-reduce.49.cloned.1.call-done = (bf16[2,1536,384]{1,2,0:T(8,128)(2,1)}, bf16[2,1536,384]{1,2,0:T(8,128)(2,1)}, bf16[2,1536,32]{1,2,0:T(8,128)(2,1)}, bf16[2,384,1536]{2,1,0:T(8,128)(2,1)}) async-done(((bf16[2,1536,384]{1,2,0:T(8,128)(2,1)}, bf16[2,1536,384]{1,2,0:T(8,128)(2,1)}, bf16[2,1536,32]{1,2,0:T(8,128)(2,1)}, bf16[2,384,1536]{2,1,0:T(8,128)(2,1)}), (bf16[2,1536,384]{1,2,0:T(8,128)(2,1)}, ...) | async-done | bytes 7274512 | tf_op jit(solution)/shard_map/psum | solution.py:108
  (1017 shorter events, 462.0 us)
Async XLA Ops:
  7.2 70.5 %all-gather.6.cloned.1.call-start = ((), (), s32[]{:S(2)}) async-start(), calls=%async_computation.6 | async-start | bytes 3538944 | tf_op jit(solution)/shard_map/all_gather | solution.py:155
  8.1 324.5 %copy-start.74 = (f32[1536]{0:T(1024)}, f32[1536]{0:T(1024)S(1)}, u32[]{:S(2)}) copy-start(f32[1536]{0:T(1024)S(1)} %get-tuple-element.1348) | copy-start | bytes 18436
  11.9 318.9 %reduce-scatter.7.cloned.1.call-start = ((), (), s32[]{:S(2)}) async-start(), calls=%async_computation.7 | async-start | bytes 7077888 | tf_op jit(solution)/shard_map/reduce_scatter | solution.py:180
  14.1 184.3 %copy-start.101 = (f32[384]{0:T(512)}, f32[384]{0:T(512)S(1)}, u32[]{:S(2)}) copy-start(f32[384]{0:T(512)S(1)} %mul.1482) | copy-start | bytes 4612
  14.7 203.3 %copy-start.106 = (f32[384]{0:T(512)}, f32[384]{0:T(512)S(1)}, u32[]{:S(2)}) copy-start(f32[384]{0:T(512)S(1)} %get-tuple-element.1351) | copy-start | bytes 4612
  14.7 550.7 %copy-start.109 = (f32[384]{0:T(512)}, f32[384]{0:T(512)S(1)}, u32[]{:S(2)}) copy-start(f32[384]{0:T(512)S(1)} %get-tuple-element.1350) | copy-start | bytes 4612
  15.4 100.9 %copy-start.111 = (f32[384]{0:T(512)}, f32[384]{0:T(512)S(1)}, u32[]{:S(2)}) copy-start(f32[384]{0:T(512)S(1)} %get-tuple-element.1342) | copy-start | bytes 4612
  15.4 100.9 %copy-start.113 = (f32[384]{0:T(512)}, f32[384]{0:T(512)S(1)}, u32[]{:S(2)}) copy-start(f32[384]{0:T(512)S(1)} %get-tuple-element.1343) | copy-start | bytes 4612
  15.4 100.9 %copy-start.115 = (f32[384]{0:T(512)}, f32[384]{0:T(512)S(1)}, u32[]{:S(2)}) copy-start(f32[384]{0:T(512)S(1)} %get-tuple-element.1344) | copy-start | bytes 4612
  15.4 100.9 %copy-start.117 = (f32[384]{0:T(512)}, f32[384]{0:T(512)S(1)}, u32[]{:S(2)}) copy-start(f32[384]{0:T(512)S(1)} %get-tuple-element.1345) | copy-start | bytes 4612
  15.4 387.5 %copy-start.119 = (f32[384]{0:T(512)}, f32[384]{0:T(512)S(1)}, u32[]{:S(2)}) copy-start(f32[384]{0:T(512)S(1)} %get-tuple-element.1340) | copy-start | bytes 4612
  15.4 387.5 %copy-start.121 = (f32[384]{0:T(512)}, f32[384]{0:T(512)S(1)}, u32[]{:S(2)}) copy-start(f32[384]{0:T(512)S(1)} %get-tuple-element.1341) | copy-start | bytes 4612
  16.6 105.9 %copy-start.158 = (f32[6]{0:T(128)}, f32[6]{0:T(128)S(1)}, u32[]{:S(2)}) copy-start(f32[6]{0:T(128)S(1)} %get-tuple-element.1585) | copy-start | bytes 76
  16.6 105.9 %copy-start.160 = (f32[6]{0:T(128)}, f32[6]{0:T(128)S(1)}, u32[]{:S(2)}) copy-start(f32[6]{0:T(128)S(1)} %get-tuple-element.1596) | copy-start | bytes 76
  17.2 94.8 %copy-start.131 = (f32[1,1,256]{2,1,0:T(1,128)}, f32[1,1,256]{2,1,0:T(1,128)S(1)}, u32[]{:S(2)}) copy-start(f32[1,1,256]{2,1,0:T(1,128)S(1)} %get-tuple-element.1568) | copy-start | bytes 3076
  17.2 94.8 %copy-start.133 = (f32[1,1,256]{2,1,0:T(1,128)}, f32[1,1,256]{2,1,0:T(1,128)S(1)}, u32[]{:S(2)}) copy-start(f32[1,1,256]{2,1,0:T(1,128)S(1)} %get-tuple-element.1569) | copy-start | bytes 3076
  17.2 94.8 %copy-start.135 = (f32[1,1,256]{2,1,0:T(1,128)}, f32[1,1,256]{2,1,0:T(1,128)S(1)}, u32[]{:S(2)}) copy-start(f32[1,1,256]{2,1,0:T(1,128)S(1)} %get-tuple-element.1570) | copy-start | bytes 3076
  17.2 94.8 %copy-start.137 = (f32[1,1,256]{2,1,0:T(1,128)}, f32[1,1,256]{2,1,0:T(1,128)S(1)}, u32[]{:S(2)}) copy-start(f32[1,1,256]{2,1,0:T(1,128)S(1)} %get-tuple-element.1571) | copy-start | bytes 3076
  223.8 107.0 %copy-start.16 = (bf16[1,128,1536]{2,1,0:T(8,128)(2,1)S(1)}, bf16[1,128,1536]{2,1,0:T(8,128)(2,1)}, u32[]{:S(2)}) copy-start(bf16[1,128,1536]{2,1,0:T(8,128)(2,1)} %param.25) | copy-start | bytes 1179652
  223.9 111.3 %copy-start.72 = (bf16[1536,32]{0,1:T(8,128)(2,1)S(1)}, bf16[1536,32]{0,1:T(8,128)(2,1)}, u32[]{:S(2)}) copy-start(bf16[1536,32]{0,1:T(8,128)(2,1)} %get-tuple-element.1560) | copy-start | bytes 294916
  223.9 171.4 %all-gather.8.cloned.1.call-start = ((), (), s32[]{:S(2)}) async-start(), calls=%async_computation.8 | async-start | bytes 3538944 | tf_op jit(solution)/shard_map/all_gather | solution.py:155
  333.9 208.6 %all-gather.12.cloned.1.call-start = ((), (), s32[]{:S(2)}) async-start(), calls=%async_computation.15 | async-start | bytes 3538944 | tf_op jit(solution)/shard_map/all_gather | solution.py:196
  334.5 491.6 %reduce-scatter.11.cloned.1.call-start = ((), (), s32[]{:S(2)}) async-start(), calls=%async_computation.10 | async-start | bytes 589824 | tf_op jit(solution)/shard_map/reduce_scatter | solution.py:216
  338.6 226.8 %copy-start.104 = (f32[384]{0:T(512)}, f32[384]{0:T(512)S(1)}, u32[]{:S(2)}) copy-start(f32[384]{0:T(512)S(1)} %mul.1530) | copy-start | bytes 4612
  744.7 167.7 %reduce-scatter.13.cloned.1.call-start = ((), (), s32[]{:S(2)}) async-start(), calls=%async_computation.11 | async-start | bytes 3538944 | tf_op jit(solution)/shard_map/reduce_scatter | solution.py:223
  833.1 79.3 %copy-start.3 = (f32[128,1536]{1,0:T(8,128)S(1)}, f32[128,1536]{1,0:T(8,128)}, u32[]{:S(2)}) copy-start(f32[128,1536]{1,0:T(8,128)} %copy-done.2) | copy-start | bytes 2359300
  833.1 79.3 %copy-start.75 = (f32[1536]{0:T(1024)S(1)}, f32[1536]{0:T(1024)}, u32[]{:S(2)}) copy-start(f32[1536]{0:T(1024)} %copy-done.74) | copy-start | bytes 18436
  833.1 79.3 %copy-start.154 = (f32[128]{0:T(128)S(1)}, f32[128]{0:T(128)}, u32[]{:S(2)}) copy-start(f32[128]{0:T(128)} %copy-done.153) | copy-start | bytes 1540
  833.1 81.1 %copy-start.30 = (bf16[1,128,1536]{2,1,0:T(8,128)(2,1)S(1)}, bf16[1,128,1536]{2,1,0:T(8,128)(2,1)}, u32[]{:S(2)}) copy-start(bf16[1,128,1536]{2,1,0:T(8,128)(2,1)} %param.26) | copy-start | bytes 1179652
  833.1 81.1 %copy-start.183 = (f32[128]{0:T(128)S(1)}, f32[128]{0:T(128)}, u32[]{:S(2)}) copy-start(f32[128]{0:T(128)} %get-tuple-element.1590) | copy-start | bytes 1540
  833.1 145.7 %copy-start.83 = (f32[1024]{0:T(1024)S(1)}, f32[1024]{0:T(1024)}, u32[]{:S(2)}) copy-start(f32[1024]{0:T(1024)} %copy-done.82) | copy-start | bytes 12292
  833.2 145.7 %copy-start.107 = (f32[384]{0:T(512)S(1)}, f32[384]{0:T(512)}, u32[]{:S(2)}) copy-start(f32[384]{0:T(512)} %copy-done.106) | copy-start | bytes 4612
  833.2 145.6 %all-gather.10.cloned.1.call-start = ((), (), s32[]{:S(2)}) async-start(), calls=%async_computation.12 | async-start | bytes 3538944 | tf_op jit(solution)/shard_map/all_gather | solution.py:196
  916.3 335.4 %reduce-scatter.15.cloned.1.call-start = ((), (), s32[]{:S(2)}) async-start(), calls=%async_computation.13 | async-start | bytes 589824 | tf_op jit(solution)/shard_map/reduce_scatter | solution.py:216
  916.6 84.0 %copy-start.6 = (f32[1024,384]{0,1:T(8,128)S(1)}, f32[1024,384]{0,1:T(8,128)}, u32[]{:S(2)}) copy-start(f32[1024,384]{0,1:T(8,128)} %copy-done.5) | copy-start | bytes 4718596
  916.6 84.0 %copy-start.102 = (f32[384]{0:T(512)S(1)}, f32[384]{0:T(512)}, u32[]{:S(2)}) copy-start(f32[384]{0:T(512)} %copy-done.101) | copy-start | bytes 4612
  916.6 84.0 %copy-start.127 = (f32[1024]{0:T(1024)S(1)}, f32[1024]{0:T(1024)}, u32[]{:S(2)}) copy-start(f32[1024]{0:T(1024)} %get-tuple-element.1574) | copy-start | bytes 12292
  1180.0 166.2 %reduce-scatter.17.cloned.1.call-start = ((), (), s32[]{:S(2)}) async-start(), calls=%async_computation.14 | async-start | bytes 3538944 | tf_op jit(solution)/shard_map/reduce_scatter | solution.py:223
  1258.3 182.1 %reduce-scatter.9.cloned.1.call-start = ((), (), s32[]{:S(2)}) async-start(), calls=%async_computation.9 | async-start | bytes 7077888 | tf_op jit(solution)/shard_map/reduce_scatter | solution.py:180
  1265.6 352.8 %all-reduce.49.cloned.1.call-start = ((), (), s32[]{:S(2)}) async-start(), calls=%async_computation.16 | async-start | bytes 14548992 | tf_op jit(solution)/shard_map/psum | solution.py:108
  1287.2 153.2 %copy-start.32 = (bf16[128,1536]{1,0:T(8,128)(2,1)S(1)}, bf16[128,1536]{1,0:T(8,128)(2,1)}, u32[]{:S(2)}) copy-start(bf16[128,1536]{1,0:T(8,128)(2,1)} %reduce-scatter.13.cloned.1.call-done) | copy-start | bytes 1179652
  1287.3 153.2 %copy-start.76 = (f32[1536]{0:T(1024)S(1)}, f32[1536]{0:T(1024)}, u32[]{:S(2)}) copy-start(f32[1536]{0:T(1024)} %copy-done.74) | copy-start | bytes 18436
  1287.3 153.2 %copy-start.155 = (f32[128]{0:T(128)S(1)}, f32[128]{0:T(128)}, u32[]{:S(2)}) copy-start(f32[128]{0:T(128)} %copy-done.153) | copy-start | bytes 1540
  1287.3 153.2 %copy-start.169 = (f32[128]{0:T(128)S(1)}, f32[128]{0:T(128)}, u32[]{:S(2)}) copy-start(f32[128]{0:T(128)} %copy-done.168) | copy-start | bytes 1540
  1287.3 153.2 %copy-start.184 = (f32[128]{0:T(128)S(1)}, f32[128]{0:T(128)}, u32[]{:S(2)}) copy-start(f32[128]{0:T(128)} %get-tuple-element.1590) | copy-start | bytes 1540
  1287.3 153.2 %copy-start.189 = (f32[128]{0:T(128)S(1)}, f32[128]{0:T(128)}, u32[]{:S(2)}) copy-start(f32[128]{0:T(128)} %get-tuple-element.1588) | copy-start | bytes 1540
  1287.3 153.2 %copy-start.4 = (f32[128,1536]{1,0:T(8,128)S(1)}, f32[128,1536]{1,0:T(8,128)}, u32[]{:S(2)}) copy-start(f32[128,1536]{1,0:T(8,128)} %copy-done.2) | copy-start | bytes 2359300
  1287.3 153.2 %copy-start.31 = (bf16[1,128,1536]{2,1,0:T(8,128)(2,1)S(1)}, bf16[1,128,1536]{2,1,0:T(8,128)(2,1)}, u32[]{:S(2)}) copy-start(bf16[1,128,1536]{2,1,0:T(8,128)(2,1)} %param.26) | copy-start | bytes 1179652
  (234 other events, 2254.2 us)
Sparse Core Ops, SparseCore 0:
  12.0 65.6 all-gather.5
  224.0 106.7 reduce-scatter.6
  334.0 61.2 all-gather.7
  397.5 62.9 all-gather.11
  744.8 81.2 reduce-scatter.10
  833.3 79.0 reduce-scatter.12
  916.4 62.3 all-gather.9
  1180.1 71.5 reduce-scatter.14
  1258.5 79.1 reduce-scatter.16
  1341.4 99.0 reduce-scatter.8
  1443.8 174.5 all-reduce.48
where the time goes:
time: 1650 us; the launch traced here: 1640 us
  waiting for transfers between devices  686 us (42%)
  local copies, waits for them, and re-layouts  310 us (19%)
  blocking collectives  254 us (15%)
  matrix products  232 us (14%)
  other arithmetic  136 us (8%)
    psum x1, waiting for transfers between devices, reduce_grads(): lax.psum(head_part[0].astype(jnp.bfloat16), 'dp').astype(jnp.float32)  175 us
    dynamic_update_slice x32, local copies, waits for them, and re-layouts, state_scan(): lax.scan(jax.checkpoint(span_scan), start_state, blocks)  159 us
    reduce_scatter x2, waiting for transfers between devices, local(): lax.psum_scatter(g_bc_full.astype(jnp.bfloat16), 'tensor', scatter_dimens...  134 us
    reduce_scatter x2, waiting for transfers between devices, local(): lax.psum_scatter(jnp.dot(gate_out, out_weight, preferred_element_type=jnp...  122 us
    all_gather x2, waiting for transfers between devices, local(): gathered = lax.all_gather(normed, 'tensor', axis=0, tiled=True)  113 us
    reduce_scatter x2, waiting for transfers between devices, local(): lax.psum_scatter(contract_cols(grad_cat, w_cat).astype(jnp.bfloat16), 'te...  79.2 us
    psum x1, blocking collectives, reduce_grads(): lax.psum((shared_part[0], shared_part[1], shared_part[2]), ('dp', 'tensor'))  77.9 us
    all_gather x2, waiting for transfers between devices, local(): lax.all_gather(grad_res.astype(jnp.bfloat16), 'tensor', axis=0, tiled=True)  62.2 us
  transfers between devices with their start and end apart: 11, of which 9 were waited for; matrix products, arithmetic and copies ran while one was open for 10% of the time, Pallas kernels for 0%

commit v1 on v0

v1 whole, which is shorter than its diff:
```python
import functools

import jax
import jax.numpy as jnp
from jax import lax
from jax.experimental import pallas as pl
from jax.experimental.pallas import tpu as pltpu
from jax.sharding import PartitionSpec as P

SPAN = 256
EPS = 1e-05
LANES = 128
VMEM_BYTES = 56 * 1024 * 1024

f32 = jnp.float32
bf16 = jnp.bfloat16
highest = lax.Precision.HIGHEST

ROWS = ((0,), (0,))
COLS = ((1,), (1,))
PLAIN = ((1,), (0,))


def dot(left, right, dims=PLAIN, precision=None):
    return lax.dot_general(
        left, right, (dims, ((), ())), preferred_element_type=f32, precision=precision
    )


def sigmoid(v):
    return 1.0 / (1.0 + jnp.exp(-v))


def softplus(v):
    return jnp.maximum(v, 0.0) + jnp.log1p(jnp.exp(-jnp.abs(v)))


def spread_heads(per_head, channels, head_dim):
    rows = per_head.shape[0]
    per_tile = LANES // head_dim
    lane = lax.broadcasted_iota(jnp.int32, (rows, LANES), 1)
    tiles = []
    for tile in range(channels // LANES):
        out = jnp.broadcast_to(
            per_head[:, tile * per_tile : tile * per_tile + 1], (rows, LANES)
        )
        for sub in range(1, per_tile):
            head = tile * per_tile + sub
            out = jnp.where(
                lane >= sub * head_dim,
                jnp.broadcast_to(per_head[:, head : head + 1], (rows, LANES)),
                out,
            )
        tiles.append(out)
    return jnp.concatenate(tiles, axis=1)


def conv_taps(buf, taps, offset, width):
    out = offset
    for j in range(4):
        out = out + taps[j : j + 1] * buf[pl.ds(5 + j, width), :]
    return out


def decay_matrix(mask, cum_col, cum_row):
    return jnp.exp(jnp.where(mask, cum_col - cum_row, -1e30))


def span_values(dt, head_ref):
    length = dt.shape[0]
    rows = lax.broadcasted_iota(jnp.int32, (length, length), 0)
    cols = lax.broadcasted_iota(jnp.int32, (length, length), 1)
    mask = rows >= cols
    pre = dt + head_ref[0:1, :]
    step = softplus(pre)
    rate = head_ref[1:2, :] * step
    cum = dot(mask.astype(f32), rate, PLAIN, highest)
    return mask, pre, step, rate, cum


def forward_kernel(
    last_layer,
    head_dim,
    *refs,
):
    if last_layer:
        (xn_ref, wz_ref, wx_ref, wbc_ref, wdt_ref, wo_ref, cx_ref, cbc_ref, head_ref, h0_ref, xt0_ref, bt0_ref, g_ref,
         z_ref, xp_ref, bc_ref, dt_ref, y_ref, hin_ref, mixed_ref, sums_ref, gg_ref, xbuf, bbuf, hst) = refs
    else:
        (xn_ref, wz_ref, wx_ref, wbc_ref, wdt_ref, wo_ref, cx_ref, cbc_ref, head_ref, h0_ref, xt0_ref, bt0_ref,
         z_ref, xp_ref, bc_ref, dt_ref, y_ref, hin_ref, mixed_ref, xbuf, bbuf, hst) = refs
    length = xn_ref.shape[0]
    channels = wz_ref.shape[1]
    state = hst.shape[0]
    width = wo_ref.shape[1]

    @pl.when(pl.program_id(0) == 0)
    def _():
        xbuf[0:8, :] = xt0_ref[...]
        bbuf[0:8, :] = bt0_ref[...]
        hst[...] = h0_ref[...]

    xn = xn_ref[...]
    z = dot(xn, wz_ref[...])
    z_ref[...] = z
    xp = dot(xn, wx_ref[...])
    xp_ref[...] = xp
    xbuf[8:, :] = xp
    bc = dot(xn, wbc_ref[...], COLS).astype(bf16)
    bc_ref[...] = bc
    bbuf[8:, :] = bc.astype(f32)
    dt = dot(xn, wdt_ref[...])
    dt_ref[...] = dt

    pre_x = conv_taps(xbuf, cx_ref[0:4, :], cx_ref[4:5, :], length)
    xc = pre_x * sigmoid(pre_x)
    pre_bc = conv_taps(bbuf, cbc_ref[0:4, :], cbc_ref[4:5, :], length)
    bcc = (pre_bc * sigmoid(pre_bc)).astype(bf16)
    xbuf[0:8, :] = xbuf[length : length + 8, :]
    bbuf[0:8, :] = bbuf[length : length + 8, :]
    b_mat = bcc[:, :state]
    c_mat = bcc[:, state:]

    mask, _, step, _, cum = span_values(dt, head_ref)
    cum_t = jnp.transpose(cum)
    scores = dot(c_mat, b_mat, COLS)
    xs = xc * spread_heads(step, channels, head_dim)
    xs_b = xs.astype(bf16)
    lane = lax.broadcasted_iota(jnp.int32, (length, LANES), 1)
    per_tile = LANES // head_dim
    tiles = []
    for tile in range(channels // LANES):
        xs_tile = xs_b[:, tile * LANES : (tile + 1) * LANES]
        out = None
        for sub in range(per_tile):
            head = tile * per_tile + sub
            decay = decay_matrix(mask, cum[:, head : head + 1], cum_t[head : head + 1, :])
            part = dot((scores * decay).astype(bf16), xs_tile)
            out = part if out is None else jnp.where(lane >= sub * head_dim, part, out)
        tiles.append(out)
    hin = hst[...]
    hin_ref[0] = hin
    last = cum[length - 1 : length, :]
    y = jnp.concatenate(tiles, axis=1)
    y = y + dot(c_mat, hin.astype(bf16)) * spread_heads(jnp.exp(cum), channels, head_dim)
    y = y + cx_ref[6:7, :] * xc
    y_ref[...] = y
    tail = spread_heads(jnp.exp(last - cum), channels, head_dim)
    keep = spread_heads(jnp.exp(last), channels, head_dim)
    hst[...] = keep * hin + dot(b_mat, (tail * xs).astype(bf16), ROWS)

    gated = y * (z * sigmoid(z))
    scaled = gated * cx_ref[5:6, :]
    mixed_ref[:, :width] = dot(scaled.astype(bf16), wo_ref[...]).astype(bf16)
    squares = jnp.sum(gated * gated, axis=1, keepdims=True)
    high = squares.astype(bf16)
    low = (squares - high.astype(f32)).astype(bf16)
    mixed_ref[:, width:] = jnp.where(
        lane == 0, high.astype(f32), jnp.where(lane == 1, low.astype(f32), 0.0)
    ).astype(bf16)
    if last_layer:
        gg = dot(g_ref[...], wo_ref[...], COLS)
        gg_ref[...] = gg
        products = jnp.sum(gg * scaled, axis=1, keepdims=True)
        both = jnp.where(lane == 0, squares, jnp.where(lane == 1, products, 0.0))
        sums_ref[...] = jnp.transpose(both)[0:8, :]


def backward_kernel(last_layer, head_dim, inner_all, *refs):
    (first_ref, tok_ref, z_ref, xp_ref, xhalo_ref, bc_ref, bchalo_ref, dt_ref, y_ref, hin_ref,
     wz_ref, wx_ref, wbc_ref, wdt_ref, wo_ref, cx_ref, cbc_ref, head_ref, pick_ref,
     dh0_ref, du0_ref, dub0_ref, xt0_ref, bt0_ref,
     go_ref, dz_ref, dx_ref, dbc_ref, ddt_ref, gn_ref, acc_ref, accbc_ref, acch_ref,
     xbuf, bbuf, dubuf, dubbuf, dhst) = refs
    length = z_ref.shape[0]
    channels = wz_ref.shape[1]
    state = dhst.shape[0]
    width = wo_ref.shape[1]
    step_id = pl.program_id(0)
    first_span = step_id == pl.num_programs(0) - 1

    @pl.when(step_id == 0)
    def _():
        dubuf[length:, :] = du0_ref[...]
        dubbuf[length:, :] = dub0_ref[...]
        dhst[...] = dh0_ref[...]
        acc_ref[...] = jnp.zeros_like(acc_ref)
        accbc_ref[...] = jnp.zeros_like(accbc_ref)
        acch_ref[...] = jnp.zeros_like(acch_ref)

    @pl.when(first_span)
    def _():
        xbuf[0:8, :] = xt0_ref[...]
        bbuf[0:8, :] = bt0_ref[...]

    @pl.when(jnp.logical_not(first_span))
    def _():
        xbuf[0:8, :] = xhalo_ref[...]
        bbuf[0:8, :] = bchalo_ref[...].astype(f32)[8:16, :]

    xbuf[8:, :] = xp_ref[...]
    bbuf[8:, :] = bc_ref[...].astype(f32)

    if last_layer:
        gg = first_ref[...]
        tok = jnp.transpose(tok_ref[...])
        rms = lax.rsqrt(tok[:, 0:1] / inner_all + EPS)
        coef = rms * rms * rms * tok[:, 1:2] / inner_all
    else:
        gg = dot(first_ref[:, :width], wo_ref[...], COLS)
        tok = first_ref[:, width:].astype(f32)
        rms = tok[:, 0:1] + tok[:, 1:2]
        coef = tok[:, 2:3] + tok[:, 3:4]
    norm_gate = cx_ref[5:6, :]
    skip = cx_ref[6:7, :]
    z = z_ref[...]
    y = y_ref[...]
    sz = sigmoid(z)
    silu_z = z * sz
    gated = y * silu_z
    rg = rms * gg
    gated_rms = gated * rms
    go_ref[...] = (gated_rms * norm_gate).astype(bf16)
    d_gated = rg * norm_gate - gated * coef
    acc_norm = jnp.sum(rg * gated, axis=0, keepdims=True)
    dz_b = (d_gated * y * (sz * (1.0 + z * (1.0 - sz)))).astype(bf16)
    dz_ref[...] = dz_b
    dy = d_gated * silu_z

    pre_x = conv_taps(xbuf, cx_ref[0:4, :], cx_ref[4:5, :], length)
    sx = sigmoid(pre_x)
    xc = pre_x * sx
    pre_bc = conv_taps(bbuf, cbc_ref[0:4, :], cbc_ref[4:5, :], length)
    sbc = sigmoid(pre_bc)
    bcc = (pre_bc * sbc).astype(bf16)
    b_mat = bcc[:, :state]
    c_mat = bcc[:, state:]
    mask, pre_dt, step, rate, cum = span_values(dt_ref[...], head_ref)
    cum_t = jnp.transpose(cum)
    last = cum[length - 1 : length, :]
    scores = dot(c_mat, b_mat, COLS)
    step_all = spread_heads(step, channels, head_dim)
    xs = xc * step_all
    xs_b = xs.astype(bf16)
    tail = spread_heads(jnp.exp(last - cum), channels, head_dim)
    keep = spread_heads(jnp.exp(last), channels, head_dim)

    hin = hin_ref[0]
    hin_b = hin.astype(bf16)
    dh = dhst[...]
    dh_b = dh.astype(bf16)
    dye = dy * spread_heads(jnp.exp(cum), channels, head_dim)
    dye_b = dye.astype(bf16)
    txs = tail * xs
    txs_b = txs.astype(bf16)
    carried = dot(c_mat, hin_b)
    pulled = dot(b_mat, dh_b)
    d_c = dot(dye_b, hin_b, COLS)
    d_b = dot(txs_b, dh_b, COLS)
    dhst[...] = keep * dh + dot(c_mat, dye_b, ROWS)
    into = txs * pulled
    across = dye * carried - into
    at_last = jnp.sum(into, axis=0, keepdims=True) + keep * jnp.sum(hin * dh, axis=0, keepdims=True)

    dy_b = dy.astype(bf16)
    dy_t = jnp.transpose(dy).astype(bf16)
    lane = lax.broadcasted_iota(jnp.int32, (length, LANES), 1)
    per_tile = LANES // head_dim
    d_scores = jnp.zeros((length, length), f32)
    row_sums = jnp.zeros((length, LANES), f32)
    col_sums = []
    dxs_parts = []
    for head in range(channels // head_dim):
        tile, sub = divmod(head, per_tile)
        dy_tile = dy_b[:, tile * LANES : (tile + 1) * LANES]
        own = (lane >= sub * head_dim) & (lane < (sub + 1) * head_dim)
        dy_head = jnp.where(own, dy_tile, jnp.zeros_like(dy_tile))
        d_m = dot(dy_head, xs_b[:, tile * LANES : (tile + 1) * LANES], COLS)
        decay = decay_matrix(mask, cum[:, head : head + 1], cum_t[head : head + 1, :])
        dxs_parts.append(
            dot(dy_t[head * head_dim : (head + 1) * head_dim, :], (scores * decay).astype(bf16))
        )
        d_m = d_m * decay
        d_scores = d_scores + d_m
        pairs = d_m * scores
        row_sums = jnp.where(lane == head, jnp.sum(pairs, axis=1, keepdims=True), row_sums)
        col_sums.append(jnp.sum(pairs, axis=0, keepdims=True))
    heads = len(col_sums)
    col_sums = jnp.concatenate(col_sums + [jnp.zeros((LANES - heads, length), f32)], axis=0)
    dxs = jnp.transpose(jnp.concatenate(dxs_parts, axis=0)) + tail * pulled
    pick = pick_ref[...]
    d_cum = row_sums - jnp.transpose(col_sums) + dot(across, pick, PLAIN, highest)
    at_last = dot(jnp.broadcast_to(at_last, (8, channels)), pick, PLAIN, highest)[0:1, :]
    d_rate = dot(mask.astype(f32), d_cum, ROWS, highest) + at_last
    d_step = d_rate * head_ref[1:2, :] + dot(dxs * xc, pick, PLAIN, highest)
    d_dt = d_step * sigmoid(pre_dt)
    acch_ref[0:1, :] += jnp.sum(d_dt, axis=0, keepdims=True)
    acch_ref[1:2, :] += jnp.sum(d_rate * rate, axis=0, keepdims=True)
    dt_b = d_dt.astype(bf16)
    ddt_ref[...] = dt_b
    ds_b = d_scores.astype(bf16)
    d_c = d_c + dot(ds_b, b_mat)
    d_b = d_b + dot(ds_b, c_mat, ROWS)
    d_xc = dxs * step_all + skip * dy
    acc_skip = jnp.sum(dy * xc, axis=0, keepdims=True)

    d_u = d_xc * (sx * (1.0 + pre_x * (1.0 - sx)))
    d_ub = jnp.concatenate([d_b, d_c], axis=1) * (sbc * (1.0 + pre_bc * (1.0 - sbc)))
    dubuf[0:length, :] = d_u
    dubbuf[0:length, :] = d_ub
    d_x = jnp.zeros_like(d_u)
    d_bc = jnp.zeros_like(d_ub)
    acc_rows = []
    accbc_rows = []
    for j in range(4):
        d_x = d_x + cx_ref[j : j + 1, :] * dubuf[pl.ds(3 - j, length), :]
        d_bc = d_bc + cbc_ref[j : j + 1, :] * dubbuf[pl.ds(3 - j, length), :]
        acc_rows.append(jnp.sum(d_u * xbuf[pl.ds(5 + j, length), :], axis=0, keepdims=True))
        accbc_rows.append(jnp.sum(d_ub * bbuf[pl.ds(5 + j, length), :], axis=0, keepdims=True))
    dubuf[length:, :] = d_u[0:8, :]
    dubbuf[length:, :] = d_ub[0:8, :]
    zero = jnp.zeros((1, channels), f32)
    acc_ref[...] += jnp.concatenate(
        acc_rows + [jnp.sum(d_u, axis=0, keepdims=True), acc_norm, acc_skip, zero], axis=0
    )
    zero = jnp.zeros((3, d_ub.shape[1]), f32)
    accbc_ref[...] += jnp.concatenate(
        accbc_rows + [jnp.sum(d_ub, axis=0, keepdims=True), zero], axis=0
    )
    dx_b = d_x.astype(bf16)
    dbc_b = d_bc.astype(bf16)
    dx_ref[...] = dx_b
    dbc_ref[...] = dbc_b
    total = dot(dz_b, wz_ref[...], COLS) + dot(dx_b, wx_ref[...], COLS)
    total = total + dot(dbc_b, wbc_ref[...]) + dot(dt_b, wdt_ref[...], COLS)
    gn_ref[...] = total.astype(bf16)


def whole(shape):
    zeros = (0,) * len(shape)
    return pl.BlockSpec(shape, lambda i: zeros)


def span_rows(columns, rows=SPAN):
    return pl.BlockSpec((rows, columns), lambda i: (i, 0))


def run_forward(xn, weights, small, carry, head_dim, grad_rows=None):
    tokens, width = xn.shape
    channels = weights[0].shape[1]
    state = carry[0].shape[0]
    spans = tokens // SPAN
    last_layer = grad_rows is not None
    operands = [xn, *weights, *small, *carry]
    in_specs = [span_rows(width)] + [whole(v.shape) for v in operands[1:]]
    shapes = [
        jax.ShapeDtypeStruct((tokens, channels), f32),
        jax.ShapeDtypeStruct((tokens, channels), f32),
        jax.ShapeDtypeStruct((tokens, 2 * state), bf16),
        jax.ShapeDtypeStruct((tokens, LANES), f32),
        jax.ShapeDtypeStruct((tokens, channels), f32),
        jax.ShapeDtypeStruct((spans, state, channels), f32),
        jax.ShapeDtypeStruct((tokens, width + LANES), bf16),
    ]
    out_specs = [
        span_rows(channels),
        span_rows(channels),
        span_rows(2 * state),
        span_rows(LANES),
        span_rows(channels),
        pl.BlockSpec((1, state, channels), lambda i: (i, 0, 0)),
        span_rows(width + LANES),
    ]
    if last_layer:
        operands.append(grad_rows)
        in_specs.append(span_rows(width))
        shapes += [
            jax.ShapeDtypeStruct((8, tokens), f32),
            jax.ShapeDtypeStruct((tokens, channels), f32),
        ]
        out_specs += [pl.BlockSpec((8, SPAN), lambda i: (0, i)), span_rows(channels)]
    return pl.pallas_call(
        functools.partial(forward_kernel, last_layer, head_dim),
        grid=(spans,),
        in_specs=in_specs,
        out_specs=out_specs,
        out_shape=shapes,
        scratch_shapes=[
            pltpu.VMEM((SPAN + 8, channels), f32),
            pltpu.VMEM((SPAN + 8, 2 * state), f32),
            pltpu.VMEM((state, channels), f32),
        ],
        compiler_params=pltpu.CompilerParams(
            dimension_semantics=("arbitrary",), vmem_limit_bytes=VMEM_BYTES
        ),
        name="layer_forward",
    )(*operands)


def run_backward(first, sums, kept, weights, small, pick, carry, head_dim, inner_all):
    z, xp, bc, dt, y, hin = kept
    tokens, channels = z.shape
    state = hin.shape[1]
    width = weights[4].shape[1]
    spans = tokens // SPAN
    last_layer = sums is not None
    if sums is None:
        sums = jnp.zeros((8, tokens), f32)

    def rev(columns, rows=SPAN):
        return pl.BlockSpec((rows, columns), lambda i: (spans - 1 - i, 0))

    def halo(columns, rows):
        per = SPAN // rows
        return pl.BlockSpec(
            (rows, columns), lambda i: (jnp.maximum((spans - 1 - i) * per - 1, 0), 0)
        )

    operands = [first, sums, z, xp, xp, bc, bc, dt, y, hin, *weights, *small, pick, *carry]
    in_specs = [
        rev(first.shape[1]),
        pl.BlockSpec((8, SPAN), lambda i: (0, spans - 1 - i)),
        rev(channels),
        rev(channels),
        halo(channels, 8),
        rev(2 * state),
        halo(2 * state, 16),
        rev(LANES),
        rev(channels),
        pl.BlockSpec((1, state, channels), lambda i: (spans - 1 - i, 0, 0)),
    ]
    in_specs += [whole(v.shape) for v in operands[len(in_specs) :]]
    shapes = [
        jax.ShapeDtypeStruct((tokens, channels), bf16),
        jax.ShapeDtypeStruct((tokens, channels), bf16),
        jax.ShapeDtypeStruct((tokens, channels), bf16),
        jax.ShapeDtypeStruct((tokens, 2 * state), bf16),
        jax.ShapeDtypeStruct((tokens, LANES), bf16),
        jax.ShapeDtypeStruct((tokens, width), bf16),
        jax.ShapeDtypeStruct((8, channels), f32),
        jax.ShapeDtypeStruct((8, 2 * state), f32),
        jax.ShapeDtypeStruct((8, LANES), f32),
    ]
    out_specs = [rev(s.shape[1]) for s in shapes[:6]] + [whole(s.shape) for s in shapes[6:]]
    return pl.pallas_call(
        functools.partial(backward_kernel, last_layer, head_dim, inner_all),
        grid=(spans,),
        in_specs=in_specs,
        out_specs=out_specs,
        out_shape=shapes,
        scratch_shapes=[
            pltpu.VMEM((SPAN + 8, channels), f32),
            pltpu.VMEM((SPAN + 8, 2 * state), f32),
            pltpu.VMEM((SPAN + 8, channels), f32),
            pltpu.VMEM((SPAN + 8, 2 * state), f32),
            pltpu.VMEM((state, channels), f32),
        ],
        compiler_params=pltpu.CompilerParams(
            dimension_semantics=("arbitrary",), vmem_limit_bytes=VMEM_BYTES
        ),
        name="layer_backward",
    )(*operands)


HIGH, DEEP = 2, 4
TENSOR_MOVES = [(dy, dz) for dy in range(HIGH) for dz in range(DEEP) if (dy, dz) != (0, 0)]


def tensor_index(y, z):
    return (y % HIGH) * DEEP + z % DEEP


def tensor_send(v, dy, dz):
    pairs = [
        (tensor_index(y, z), tensor_index(y + dy, z + dz))
        for y in range(HIGH)
        for z in range(DEEP)
    ]
    return lax.ppermute(v, "tensor", pairs)


def place():
    me = lax.axis_index("tensor")
    return me, me // DEEP, me % DEEP


def gather_tensor(v):
    me, y, z = place()
    out = jnp.zeros((HIGH * DEEP,) + v.shape, v.dtype)
    out = lax.dynamic_update_index_in_dim(out, v, me, 0)
    for dy, dz in TENSOR_MOVES:
        source = ((y - dy) % HIGH) * DEEP + (z - dz) % DEEP
        out = lax.dynamic_update_index_in_dim(out, tensor_send(v, dy, dz), source, 0)
    return out


def scatter_tensor(v):
    me, y, z = place()
    blocks = v.reshape((HIGH * DEEP, v.shape[0] // (HIGH * DEEP)) + v.shape[1:])
    total = lax.dynamic_index_in_dim(blocks, me, 0, False).astype(f32)
    for dy, dz in TENSOR_MOVES:
        target = ((y + dy) % HIGH) * DEEP + (z + dz) % DEEP
        block = lax.dynamic_index_in_dim(blocks, target, 0, False)
        total = total + tensor_send(block, dy, dz).astype(f32)
    return total


def sum_tensor(v):
    total = v
    for dy, dz in TENSOR_MOVES:
        total = total + tensor_send(v, dy, dz)
    return total


def pad_lanes(v, lanes=LANES):
    return jnp.pad(v, [(0, 0)] * (v.ndim - 1) + [(0, lanes - v.shape[-1])])


def split_two(v):
    high = v.astype(bf16)
    return high, (v - high.astype(f32)).astype(bf16)


def local(
    hidden_in,
    grad_out,
    norm_in,
    w_z,
    w_x,
    w_bc,
    w_dt,
    conv_x,
    conv_x_bias,
    conv_bc,
    conv_bc_bias,
    dt_bias,
    a_log,
    skip,
    norm_gate,
    w_out,
):
    layers, width, channels = w_z.shape
    heads = w_dt.shape[2]
    head_dim = channels // heads
    both = conv_bc.shape[2]
    state = both // 2
    inner_all = channels * lax.axis_size("tensor")
    rows = hidden_in.shape[1]
    tokens = rows * lax.axis_size("tensor")

    residual = hidden_in[0].astype(f32)
    grad_res = grad_out[0].astype(f32)

    def normalize(v, gain):
        inv = lax.rsqrt(jnp.mean(v * v, axis=-1, keepdims=True) + EPS)
        return inv, (v * inv * gain[None, :]).astype(bf16)

    inv_rms, normed = normalize(residual, norm_in[0])
    gathered = gather_tensor(normed).reshape(tokens, width)

    bc_rows = jnp.swapaxes(w_bc, 1, 2)
    bc_rows = gather_tensor(bc_rows)
    bc_rows = jnp.swapaxes(bc_rows, 0, 1).reshape(layers, both, width)
    grad_rows = gather_tensor(grad_out[0]).reshape(tokens, width)

    channel_head = jnp.arange(channels) // head_dim
    pick = (channel_head[:, None] == jnp.arange(LANES)[None, :]).astype(f32)
    zero_row = jnp.zeros((1, channels), f32)
    weights, smalls = [], []
    for layer in range(layers):
        weights.append((w_z[layer], w_x[layer], bc_rows[layer], pad_lanes(w_dt[layer]), w_out[layer]))
        skip_all = jnp.repeat(skip[layer], head_dim)
        cx = jnp.concatenate(
            [conv_x[layer], conv_x_bias[layer][None], norm_gate[layer][None], skip_all[None], zero_row],
            axis=0,
        )
        cbc = jnp.concatenate(
            [conv_bc[layer], conv_bc_bias[layer][None], jnp.zeros((3, both), f32)], axis=0
        )
        head = jnp.concatenate(
            [
                pad_lanes(dt_bias[layer][None]),
                pad_lanes(-jnp.exp(a_log[layer])[None]),
                jnp.zeros((6, LANES), f32),
            ],
            axis=0,
        )
        smalls.append((cx, cbc, head))
    zero_state = jnp.zeros((state, channels), f32)
    zero_x = jnp.zeros((8, channels), f32)
    zero_bc = jnp.zeros((8, both), f32)
    carry = (zero_state, zero_x, zero_bc)

    kept = []
    for layer in range(layers):
        last = layer == layers - 1
        out = run_forward(
            gathered, weights[layer], smalls[layer], carry, head_dim, grad_rows if last else None
        )
        mixed = scatter_tensor(out[6])
        squares = mixed[:, width : width + 1] + mixed[:, width + 1 : width + 2]
        gate_rms = lax.rsqrt(squares / inner_all + EPS)
        mixed = mixed[:, :width] * gate_rms
        kept.append((residual, inv_rms, gathered, out, gate_rms, mixed))
        residual = residual + mixed
        if not last:
            inv_rms, normed = normalize(residual, norm_in[layer + 1])
            gathered = gather_tensor(normed).reshape(tokens, width)

    head_parts = [None] * layers
    shared_parts = [None] * layers
    for layer in reversed(range(layers)):
        res_in, inv_rms, gathered, out, gate_rms, mixed = kept[layer]
        if layer == layers - 1:
            sums = sum_tensor(out[7])
            first = out[8]
        else:
            sums = None
            g_mixed = grad_res.astype(bf16)
            products = jnp.sum(g_mixed.astype(f32) * mixed, axis=-1, keepdims=True)
            coef = gate_rms * gate_rms * products / inner_all
            extra = jnp.concatenate([*split_two(gate_rms), *split_two(coef)], axis=1)
            sent = jnp.concatenate([g_mixed, pad_lanes(extra)], axis=1)
            first = gather_tensor(sent).reshape(tokens, width + LANES)
            grad_rows = first[:, :width]
        back = run_backward(
            first, sums, out[:6], weights[layer], smalls[layer], pick,
            (zero_state, zero_x, zero_bc, zero_x, zero_bc), head_dim, inner_all,
        )
        gate_out, dz, dx, dbc, ddt, gn, acc, accbc, acch = back
        grad_normed = scatter_tensor(gn)
        scaled = grad_normed * norm_in[layer][None, :]
        g_norm_in = jnp.sum(grad_normed * res_in * inv_rms, axis=0)
        grad_res = (
            grad_res
            + inv_rms * scaled
            - res_in
            * inv_rms**3
            * (jnp.sum(scaled * res_in, axis=-1, keepdims=True) / width)
        )
        bc_sum = scatter_tensor(jnp.transpose(dbc)).astype(bf16)
        head_parts[layer] = (
            dot(gathered, dz, ROWS),
            dot(gathered, dx, ROWS),
            dot(bc_sum, gathered),
            dot(gathered, ddt, ROWS)[:, :heads],
            acc[0:4],
            acc[4],
            acch[0, :heads],
            acch[1, :heads],
            jnp.sum(acc[6].reshape(heads, head_dim), axis=1),
            acc[5],
            dot(gate_out, grad_rows, ROWS),
        )
        shared_parts[layer] = (g_norm_in, accbc[0:4], accbc[4])

    big = (0, 1, 2, 10)
    head_sums = [None] * layers
    for layer in reversed(range(layers)):
        sums_big = lax.psum(tuple(head_parts[layer][i].astype(bf16) for i in big), "dp")
        head_sums[layer] = {i: v.astype(f32) for i, v in zip(big, sums_big)}
    little = tuple(
        jnp.stack([head_parts[layer][i] for layer in range(layers)])
        for i in range(11)
        if i not in big
    )
    little = lax.psum(little, "dp")
    shared = tuple(
        jnp.stack([shared_parts[layer][i] for layer in range(layers)]) for i in range(3)
    )
    shared = lax.psum(shared, ("dp", "tensor"))
    g_wz, g_wx, g_wbc, g_wo = (
        jnp.stack([head_sums[layer][i] for layer in range(layers)]) for i in big
    )
    g_wdt, g_cx, g_cxb, g_dtb, g_alog, g_skip, g_ng = little
    return (
        residual[None],
        grad_res[None],
        shared[0],
        g_wz,
        g_wx,
        jnp.swapaxes(g_wbc, 1, 2),
        g_wdt,
        g_cx,
        g_cxb,
        shared[1],
        shared[2],
        g_dtb,
        g_alog,
        g_skip,
        g_ng,
        g_wo,
    )


def solution(mesh):
    specs_in = (
        P("dp", "tensor", None),
        P("dp", "tensor", None),
        P(),
        P(None, None, "tensor"),
        P(None, None, "tensor"),
        P(None, None, "tensor"),
        P(None, None, "tensor"),
        P(None, None, "tensor"),
        P(None, "tensor"),
        P(),
        P(),
        P(None, "tensor"),
        P(None, "tensor"),
        P(None, "tensor"),
        P(None, "tensor"),
        P(None, "tensor", None),
    )
    specs_out = (
        P("dp", "tensor", None),
        P("dp", "tensor", None),
        P(),
        P(None, None, "tensor"),
        P(None, None, "tensor"),
        P(None, None, "tensor"),
        P(None, None, "tensor"),
        P(None, None, "tensor"),
        P(None, "tensor"),
        P(),
        P(),
        P(None, "tensor"),
        P(None, "tensor"),
        P(None, "tensor"),
        P(None, "tensor"),
        P(None, "tensor", None),
    )
    return jax.shard_map(
        local, mesh=mesh, in_specs=specs_in, out_specs=specs_out, check_vma=False
    )
```

time: 1650 us -> 824 us (0.50)
  waiting for transfers between devices: 686 us -> 124 us
  matrix products: 232 us -> 29.2 us
  starting transfers between devices: 1.61 us -> 155 us
  local copies, waits for them, and re-layouts: 310 us -> 183 us
  other arithmetic: 136 us -> 35.3 us
  Pallas kernels: 0 us -> 96.2 us
  blocking collectives: 254 us -> 175 us
    reduce_scatter x6 -> x0, waiting for transfers between devices: 335 us -> none  [the longest x2 134 us: local(): lax.psum_scatter(g_bc_full.astype(jnp.bfloat16), 'tensor', scatter_dimens...]
    dot_general x148 -> x10, matrix products: 232 us -> 29.2 us  [dot(): lax.dot_general(left, right, (dims, ((), ())), preferred_element_type=f32...]
    all_gather x4 -> x0, waiting for transfers between devices: 175 us -> none  [the longest x2 113 us: local(): gathered = lax.all_gather(normed, 'tensor', axis=0, tiled=True)]
    ppermute x0 -> x84, starting transfers between devices: none -> 155 us  [tensor_send(): return lax.ppermute(v, 'tensor', pairs)]
    dynamic_update_slice x32 -> x39, local copies, waits for them, and re-layouts: 159 us -> 32.5 us  [the longest x34 29.2 us: gather_tensor(): lax.dynamic_update_index_in_dim(out, tensor_send(v, dy, dz), source, 0)]
    psum x1 -> x2, waiting for transfers between devices: 175 us -> 64.9 us  [the longest x1 64.8 us: local(): lax.psum(tuple((head_parts[layer][i].astype(bf16) for i in big)), 'dp')]
    pallas_call x0 -> x4, Pallas kernels: none -> 96.2 us  [the longest x2 56.1 us: run_backward(): pl.pallas_call(functools.partial(backward_kernel, last_layer, head_dim, i...]
    all_gather x2 -> x0, blocking collectives: 59.6 us -> none  [local(): lax.all_gather(bc_part, 'tensor', axis=1, tiled=True).astype(jnp.float32)]
  transfers between devices with their start and end apart: 11 -> 86, of which waited for: 9 -> 22; matrix products, arithmetic and copies ran while one was open for 10% -> 25% of each run, Pallas kernels for 0% -> 2%
where the time goes in v1:
time: 824 us; the launch traced here: 812 us
  local copies, waits for them, and re-layouts  183 us (22%)
  blocking collectives  175 us (21%)
  starting transfers between devices  155 us (19%)
  waiting for transfers between devices  124 us (15%)
  Pallas kernels  96.2 us (12%)
  other arithmetic  35.3 us (4%)
  matrix products  29.2 us (4%)
  between operations  15.5 us (2%)
    ppermute x84, starting transfers between devices, tensor_send(): return lax.ppermute(v, 'tensor', pairs)  155 us
    psum x1, blocking collectives, local(): little = lax.psum(little, 'dp')  102 us
    psum x1, blocking collectives, local(): shared = lax.psum(shared, ('dp', 'tensor'))  72.2 us
    psum x1, waiting for transfers between devices, local(): lax.psum(tuple((head_parts[layer][i].astype(bf16) for i in big)), 'dp')  64.8 us
    ppermute x84, waiting for transfers between devices, tensor_send(): return lax.ppermute(v, 'tensor', pairs)  58.6 us
    pallas_call x2, Pallas kernels, run_backward(): pl.pallas_call(functools.partial(backward_kernel, last_layer, head_dim, i...  56.1 us
    broadcast_in_dim x28, local copies, waits for them, and re-layouts, gather_tensor(): lax.dynamic_update_index_in_dim(out, tensor_send(v, dy, dz), source, 0)  42.5 us
    pallas_call x2, Pallas kernels, run_forward(): pl.pallas_call(functools.partial(forward_kernel, last_layer, head_dim), g...  40.1 us
  transfers between devices with their start and end apart: 86, of which 22 were waited for; matrix products, arithmetic and copies ran while one was open for 25% of the time, Pallas kernels for 2%

profile of v1, /device:TPU:1, one launch (start us, length us, event | category | flops | bytes accessed | tf_op | source)
XLA Modules:
  0.0 811.9 jit_solution(14996150454613332155)
XLA Ops:
  9.9 3.3 collective-permute-start.8
  13.9 2.9 collective-permute-start.10
  53.7 3.1 collective-permute-start.12
  70.5 3.0 collective-permute-start.3
  74.9 3.6 collective-permute-start.5
  86.9 5.4 collective-permute-start.28
  104.0 4.3 collective-permute-start.32
  114.6 2.9 collective-permute-start.33
  118.4 3.3 collective-permute-start.34
  124.0 18.7 %layer_forward.2 = (f32[1024,384]{1,0:T(8,128)}, f32[1024,384]{1,0:T(8,128)}, bf16[1024,256]{1,0:T(8,128)(2,1)}, f32[1024,128]{1,0:T(8,128)}, f32[1024,384]{1,0:...) custom-call(bf16[1024,1536]{1,0:T(8,128)(2,1)} %bitcast.291, ...), custom_call_target="tpu_custom_call" | custom-call | tf_op jit(solution)/shard_map/layer_forward/pallas_call | solution.py:382
  142.7 3.0 constant_dynamic-slice_fusion.31
  156.2 3.3 collective-permute-start.14
  174.9 3.3 collective-permute-start.20
  180.0 5.3 collective-permute-done.19
  185.3 10.3 %collective-permute-done.20 = bf16[128,1664]{0,1:T(8,128)(2,1)S(1)} collective-permute-done((bf16[128,1664]{0,1:T(8,128)(2,1)}, bf16[128,1664]{0,1:T(8,128)(2,1)S(1)}, u32[]{:S(2)}, u32[]{:S(2)}) %collective-permute-start.20) | collective-permute-done | bytes 426016 | tf_op jit(solution)/shard_map/ppermute | solution.py:479
  209.0 6.0 collective-permute-start.26
  239.4 21.4 %layer_forward.3 = (f32[1024,384]{1,0:T(8,128)}, f32[1024,384]{1,0:T(8,128)}, bf16[1024,256]{1,0:T(8,128)(2,1)}, f32[1024,128]{1,0:T(8,128)}, f32[1024,384]{1,0:...) custom-call(bf16[1024,1536]{1,0:T(8,128)(2,1)} %bitcast.296, ...), custom_call_target="tpu_custom_call" | custom-call | tf_op jit(solution)/shard_map/layer_forward/pallas_call | solution.py:382
  261.8 3.1 collective-permute-start.43
  264.9 3.0 collective-permute-start.45
  278.8 27.4 %layer_backward.2 = (bf16[1024,384]{1,0:T(8,128)(2,1)}, bf16[1024,384]{1,0:T(8,128)(2,1)}, bf16[1024,384]{1,0:T(8,128)(2,1)}, bf16[1024,256]{1,0:T(8,128)(2,1)},...) custom-call(f32[1024,384]{1,0:T(8,128)} %get-tuple-element.52.refs_0, ...), custom_call_target="tpu_custom_call" | custom-call | tf_op jit(solution)/shard_map/layer_backward/pallas_call | solution.py:445
  306.2 3.1 constant_dynamic-slice_fusion.15
  321.2 3.2 collective-permute-start.53
  333.3 4.1 fusion.8
  338.1 4.1 collective-permute-start.55
  350.8 7.5 collective-permute-done.55
  364.7 4.4 fusion.9
  370.2 4.9 collective-permute-start.82
  377.7 3.7 collective-permute-start.59
  382.7 4.4 collective-permute-start.61
  400.4 3.2 collective-permute-done.62
  411.0 28.7 %layer_backward.3 = (bf16[1024,384]{1,0:T(8,128)(2,1)}, bf16[1024,384]{1,0:T(8,128)(2,1)}, bf16[1024,384]{1,0:T(8,128)(2,1)}, bf16[1024,256]{1,0:T(8,128)(2,1)},...) custom-call(bf16[1024,1664]{1,0:T(8,128)(2,1)} %bitcast.100.refs_0_,, ...), custom_call_target="tpu_custom_call" | custom-call | tf_op jit(solution)/shard_map/layer_backward/pallas_call | solution.py:445
  439.7 4.7 fusion.10
  449.0 3.7 collective-permute-start.71
  452.7 2.9 collective-permute-start.73
  457.1 4.1 fusion.7
  464.5 3.1 collective-permute-start.75
  475.9 3.0 constant_dynamic-slice_fusion.23
  495.5 4.0 collective-permute-start.41
  502.7 5.1 collective-permute-done.40
  507.8 4.2 collective-permute-done.41
  513.7 3.0 constant_dynamic-slice_fusion.7
  520.9 3.1 collective-permute-start.64
  528.0 3.2 collective-permute-start.67
  537.2 5.2 collective-permute-done.64
  543.6 102.3 %all-reduce.8 = (f32[2,4,384]{2,1,0:T(4,128)}, f32[2,384]{1,0:T(2,128)}, f32[2,6]{1,0:T(2,128)}, f32[2,6]{1,0:T(2,128)}, f32[2,6]{1,0:T(2,128)}, /*index=5*/f32[2,384]{1,0:T(2,128)}) all-reduce(f32[2,4,384]{2,1,0:T(4,128)S(1)} %pad_maximum_fusion.3, f32[2,384]{1,0:T(2,128)S(1)} %pad_maximum_fusion.5, ...), channel_id=1, replica_groups=mesh['dp'=16,'tensor'=8] {'dp'}, use_global_device_ids=true, to_apply=%region_15.16 | all-reduce | flops 4644 | bytes 37152 | tf_op jit(solution)/shard_map/psum | solution.py:667
  657.4 72.2 %all-reduce.7 = (f32[2,1536]{1,0:T(2,128)}, f32[2,4,256]{2,1,0:T(4,128)}, f32[2,256]{1,0:T(2,128)}) all-reduce(f32[2,1536]{1,0:T(2,128)S(1)} %pad_maximum_fusion.2, f32[2,4,256]{2,1,0:T(4,128)S(1)} %pad_maximum_fusion.4, f32[2,256]{1,0:T(2,128)S(1)} %pad_maximum_fusion.7), channel_id=1, replica_groups=mesh['dp'=16,'tensor'=8] {'dp','tensor'}, use_global_device_ids=true, to_apply=%region_7.8 | all-reduce | flops 5632 | bytes 45056 | tf_op jit(solution)/shard_map/psum | solution.py:671
  729.6 64.8 %all-reduce.15.cloned.1.call-done = (bf16[1,1536,384]{2,1,0:T(8,128)(2,1)}, bf16[1,1536,384]{2,1,0:T(8,128)(2,1)}, bf16[1,1536,384]{2,1,0:T(8,128)(2,1)}, bf16[1...) async-done(((bf16[1,1536,384]{2,1,0:T(8,128)(2,1)}, ...) | async-done | bytes 7274512 | tf_op jit(solution)/shard_map/psum | solution.py:660
  794.5 4.3 maximum_convert_fusion.2
  (495 shorter events, 295.5 us)
Async XLA Ops:
  7.3 638.7 %all-reduce.13.cloned.1.call-start = ((), (), s32[]{:S(2)}) async-start(), calls=%async_computation | async-start | bytes 196608 | tf_op jit(solution)/shard_map/psum | solution.py:667
  7.3 46.3 %collective-permute-start.7 = (bf16[2,32,1536]{2,1,0:T(8,128)(2,1)}, bf16[2,32,1536]{2,1,0:T(8,128)(2,1)}, u32[]{:S(2)}, u32[]{:S(2)}) collective-permute-start(bf16[2,32,1536]{2,1,0:T(8,128)(2,1)} %bitcast.345), channel_id=1, source_target_pairs={{0,1},{1,2},{2,3},{3,0},{4,5},{5,6},{6,7},{7,4},{8,9},{9,10},{10,1... | collective-permute-start | bytes 589832 | tf_op jit(solution)/shard_map/ppermute | solution.py:479
  9.9 48.5 %collective-permute-start.8 = (bf16[2,32,1536]{2,1,0:T(8,128)(2,1)}, bf16[2,32,1536]{2,1,0:T(8,128)(2,1)}, u32[]{:S(2)}, u32[]{:S(2)}) collective-permute-start(bf16[2,32,1536]{2,1,0:T(8,128)(2,1)} %bitcast.346), channel_id=1, source_target_pairs={{0,2},{1,3},{2,0},{3,1},{4,6},{5,7},{6,4},{7,5},{8,10},{9,11},{10,... | collective-permute-start | bytes 589832 | tf_op jit(solution)/shard_map/ppermute | solution.py:479
  13.2 48.8 %collective-permute-start.9 = (bf16[2,32,1536]{2,1,0:T(8,128)(2,1)}, bf16[2,32,1536]{2,1,0:T(8,128)(2,1)}, u32[]{:S(2)}, u32[]{:S(2)}) collective-permute-start(bf16[2,32,1536]{2,1,0:T(8,128)(2,1)} %bitcast.347), channel_id=1, source_target_pairs={{0,3},{1,0},{2,1},{3,2},{4,7},{5,4},{6,5},{7,6},{8,11},{9,8},{10,9... | collective-permute-start | bytes 589832 | tf_op jit(solution)/shard_map/ppermute | solution.py:479
  13.9 49.8 %collective-permute-start.10 = (bf16[2,32,1536]{2,1,0:T(8,128)(2,1)}, bf16[2,32,1536]{2,1,0:T(8,128)(2,1)}, u32[]{:S(2)}, u32[]{:S(2)}) collective-permute-start(bf16[2,32,1536]{2,1,0:T(8,128)(2,1)} %bitcast.348), channel_id=1, source_target_pairs={{0,4},{1,5},{2,6},{3,7},{4,0},{5,1},{6,2},{7,3},{8,12},{9,13},{10,... | collective-permute-start | bytes 589832 | tf_op jit(solution)/shard_map/ppermute | solution.py:479
  16.8 50.2 %collective-permute-start.11 = (bf16[2,32,1536]{2,1,0:T(8,128)(2,1)}, bf16[2,32,1536]{2,1,0:T(8,128)(2,1)}, u32[]{:S(2)}, u32[]{:S(2)}) collective-permute-start(bf16[2,32,1536]{2,1,0:T(8,128)(2,1)} %bitcast.349), channel_id=1, source_target_pairs={{0,5},{1,6},{2,7},{3,4},{4,1},{5,2},{6,3},{7,0},{8,13},{9,14},{10,... | collective-permute-start | bytes 589832 | tf_op jit(solution)/shard_map/ppermute | solution.py:479
  53.7 16.9 %collective-permute-start.12 = (bf16[2,32,1536]{2,1,0:T(8,128)(2,1)}, bf16[2,32,1536]{2,1,0:T(8,128)(2,1)S(1)}, u32[]{:S(2)}, u32[]{:S(2)}) collective-permute-start(bf16[2,32,1536]{2,1,0:T(8,128)(2,1)} %bitcast.350), channel_id=1, source_target_pairs={{0,6},{1,7},{2,4},{3,5},{4,2},{5,3},{6,0},{7,1},{8,14},{9,15},{10,... | collective-permute-start | bytes 589832 | tf_op jit(solution)/shard_map/ppermute | solution.py:479
  67.0 19.9 %collective-permute-start.2 = (bf16[128,1536]{0,1:T(8,128)(2,1)}, bf16[128,1536]{0,1:T(8,128)(2,1)}, u32[]{:S(2)}, u32[]{:S(2)}) collective-permute-start(bf16[128,1536]{0,1:T(8,128)(2,1)} %fusion.35), channel_id=1, source_target_pairs={{0,3},{1,0},{2,1},{3,2},{4,7},{5,4},{6,5},{7,6},{8,11},{9,8},{10,9... | collective-permute-start | bytes 1179656 | tf_op jit(solution)/shard_map/ppermute | solution.py:479
  70.5 23.6 %collective-permute-start.3 = (bf16[128,1536]{0,1:T(8,128)(2,1)}, bf16[128,1536]{0,1:T(8,128)(2,1)}, u32[]{:S(2)}, u32[]{:S(2)}) collective-permute-start(bf16[128,1536]{0,1:T(8,128)(2,1)} %fusion.35), channel_id=1, source_target_pairs={{0,4},{1,5},{2,6},{3,7},{4,0},{5,1},{6,2},{7,3},{8,12},{9,13},{10,... | collective-permute-start | bytes 1179656 | tf_op jit(solution)/shard_map/ppermute | solution.py:479
  74.2 21.9 %collective-permute-start.4 = (bf16[128,1536]{0,1:T(8,128)(2,1)}, bf16[128,1536]{0,1:T(8,128)(2,1)}, u32[]{:S(2)}, u32[]{:S(2)}) collective-permute-start(bf16[128,1536]{0,1:T(8,128)(2,1)} %fusion.35), channel_id=1, source_target_pairs={{0,5},{1,6},{2,7},{3,4},{4,1},{5,2},{6,3},{7,0},{8,13},{9,14},{10,... | collective-permute-start | bytes 1179656 | tf_op jit(solution)/shard_map/ppermute | solution.py:479
  74.9 25.5 %collective-permute-start.5 = (bf16[128,1536]{0,1:T(8,128)(2,1)}, bf16[128,1536]{0,1:T(8,128)(2,1)}, u32[]{:S(2)}, u32[]{:S(2)}) collective-permute-start(bf16[128,1536]{0,1:T(8,128)(2,1)} %fusion.35), channel_id=1, source_target_pairs={{0,6},{1,7},{2,4},{3,5},{4,2},{5,3},{6,0},{7,1},{8,14},{9,15},{10,... | collective-permute-start | bytes 1179656 | tf_op jit(solution)/shard_map/ppermute | solution.py:479
  79.0 25.0 %collective-permute-start.6 = (bf16[128,1536]{0,1:T(8,128)(2,1)}, bf16[128,1536]{0,1:T(8,128)(2,1)}, u32[]{:S(2)}, u32[]{:S(2)}) collective-permute-start(bf16[128,1536]{0,1:T(8,128)(2,1)} %fusion.35), channel_id=1, source_target_pairs={{0,7},{1,4},{2,5},{3,6},{4,3},{5,0},{6,1},{7,2},{8,15},{9,12},{10,... | collective-permute-start | bytes 1179656 | tf_op jit(solution)/shard_map/ppermute | solution.py:479
  86.9 27.8 %collective-permute-start.28 = (bf16[128,1536]{0,1:T(8,128)(2,1)}, bf16[128,1536]{0,1:T(8,128)(2,1)}, u32[]{:S(2)}, u32[]{:S(2)}) collective-permute-start(bf16[128,1536]{0,1:T(8,128)(2,1)} %bitcast.62), channel_id=1, source_target_pairs={{0,1},{1,2},{2,3},{3,0},{4,5},{5,6},{6,7},{7,4},{8,9},{9,10},{10,1... | collective-permute-start | bytes 1179656 | tf_op jit(solution)/shard_map/ppermute | solution.py:479
  94.2 24.2 %collective-permute-start.29 = (bf16[128,1536]{0,1:T(8,128)(2,1)}, bf16[128,1536]{0,1:T(8,128)(2,1)}, u32[]{:S(2)}, u32[]{:S(2)}) collective-permute-start(bf16[128,1536]{0,1:T(8,128)(2,1)} %bitcast.62), channel_id=1, source_target_pairs={{0,2},{1,3},{2,0},{3,1},{4,6},{5,7},{6,4},{7,5},{8,10},{9,11},{10,... | collective-permute-start | bytes 1179656 | tf_op jit(solution)/shard_map/ppermute | solution.py:479
  96.1 60.1 %collective-permute-start.30 = (bf16[128,1536]{0,1:T(8,128)(2,1)}, bf16[128,1536]{0,1:T(8,128)(2,1)}, u32[]{:S(2)}, u32[]{:S(2)}) collective-permute-start(bf16[128,1536]{0,1:T(8,128)(2,1)} %bitcast.62), channel_id=1, source_target_pairs={{0,3},{1,0},{2,1},{3,2},{4,7},{5,4},{6,5},{7,6},{8,11},{9,8},{10,9... | collective-permute-start | bytes 1179656 | tf_op jit(solution)/shard_map/ppermute | solution.py:479
  100.4 60.3 %collective-permute-start.31 = (bf16[128,1536]{0,1:T(8,128)(2,1)}, bf16[128,1536]{0,1:T(8,128)(2,1)}, u32[]{:S(2)}, u32[]{:S(2)}) collective-permute-start(bf16[128,1536]{0,1:T(8,128)(2,1)} %bitcast.62), channel_id=1, source_target_pairs={{0,4},{1,5},{2,6},{3,7},{4,0},{5,1},{6,2},{7,3},{8,12},{9,13},{10,... | collective-permute-start | bytes 1179656 | tf_op jit(solution)/shard_map/ppermute | solution.py:479
  104.0 57.9 %collective-permute-start.32 = (bf16[128,1536]{0,1:T(8,128)(2,1)}, bf16[128,1536]{0,1:T(8,128)(2,1)}, u32[]{:S(2)}, u32[]{:S(2)}) collective-permute-start(bf16[128,1536]{0,1:T(8,128)(2,1)} %bitcast.62), channel_id=1, source_target_pairs={{0,5},{1,6},{2,7},{3,4},{4,1},{5,2},{6,3},{7,0},{8,13},{9,14},{10,... | collective-permute-start | bytes 1179656 | tf_op jit(solution)/shard_map/ppermute | solution.py:479
  114.6 51.0 %collective-permute-start.33 = (bf16[128,1536]{0,1:T(8,128)(2,1)}, bf16[128,1536]{0,1:T(8,128)(2,1)}, u32[]{:S(2)}, u32[]{:S(2)}) collective-permute-start(bf16[128,1536]{0,1:T(8,128)(2,1)} %bitcast.62), channel_id=1, source_target_pairs={{0,6},{1,7},{2,4},{3,5},{4,2},{5,3},{6,0},{7,1},{8,14},{9,15},{10,... | collective-permute-start | bytes 1179656 | tf_op jit(solution)/shard_map/ppermute | solution.py:479
  118.4 48.5 %collective-permute-start.34 = (bf16[128,1536]{0,1:T(8,128)(2,1)}, bf16[128,1536]{0,1:T(8,128)(2,1)}, u32[]{:S(2)}, u32[]{:S(2)}) collective-permute-start(bf16[128,1536]{0,1:T(8,128)(2,1)} %bitcast.62), channel_id=1, source_target_pairs={{0,7},{1,4},{2,5},{3,6},{4,3},{5,0},{6,1},{7,2},{8,15},{9,12},{10,... | collective-permute-start | bytes 1179656 | tf_op jit(solution)/shard_map/ppermute | solution.py:479
  162.0 17.8 %collective-permute-start.16 = (bf16[128,1664]{0,1:T(8,128)(2,1)}, bf16[128,1664]{0,1:T(8,128)(2,1)}, u32[]{:S(2)}, u32[]{:S(2)}) collective-permute-start(bf16[128,1664]{0,1:T(8,128)(2,1)} %bitcast.322), channel_id=1, source_target_pairs={{0,3},{1,0},{2,1},{3,2},{4,7},{5,4},{6,5},{7,6},{8,11},{9,8},{10,9... | collective-permute-start | bytes 1277960 | tf_op jit(solution)/shard_map/ppermute | solution.py:479
  174.9 20.7 %collective-permute-start.20 = (bf16[128,1664]{0,1:T(8,128)(2,1)}, bf16[128,1664]{0,1:T(8,128)(2,1)S(1)}, u32[]{:S(2)}, u32[]{:S(2)}) collective-permute-start(bf16[128,1664]{0,1:T(8,128)(2,1)} %bitcast.317), channel_id=1, source_target_pairs={{0,7},{1,4},{2,5},{3,6},{4,3},{5,0},{6,1},{7,2},{8,15},{9,12},{10,... | collective-permute-start | bytes 1277960 | tf_op jit(solution)/shard_map/ppermute | solution.py:479
  204.7 17.1 %collective-permute-start.23 = (bf16[128,1536]{0,1:T(8,128)(2,1)}, bf16[128,1536]{0,1:T(8,128)(2,1)}, u32[]{:S(2)}, u32[]{:S(2)}) collective-permute-start(bf16[128,1536]{0,1:T(8,128)(2,1)} %multiply_convert_fusion), channel_id=1, source_target_pairs={{0,3},{1,0},{2,1},{3,2},{4,7},{5,4},{6,5},{7,6},{8,11},{9,8},{10,9... | collective-permute-start | bytes 1179656 | tf_op jit(solution)/shard_map/ppermute | solution.py:479
  206.0 17.8 %collective-permute-start.24 = (bf16[128,1536]{0,1:T(8,128)(2,1)}, bf16[128,1536]{0,1:T(8,128)(2,1)}, u32[]{:S(2)}, u32[]{:S(2)}) collective-permute-start(bf16[128,1536]{0,1:T(8,128)(2,1)} %multiply_convert_fusion), channel_id=1, source_target_pairs={{0,4},{1,5},{2,6},{3,7},{4,0},{5,1},{6,2},{7,3},{8,12},{9,13},{10,... | collective-permute-start | bytes 1179656 | tf_op jit(solution)/shard_map/ppermute | solution.py:479
  208.0 17.6 %collective-permute-start.25 = (bf16[128,1536]{0,1:T(8,128)(2,1)}, bf16[128,1536]{0,1:T(8,128)(2,1)}, u32[]{:S(2)}, u32[]{:S(2)}) collective-permute-start(bf16[128,1536]{0,1:T(8,128)(2,1)} %multiply_convert_fusion), channel_id=1, source_target_pairs={{0,5},{1,6},{2,7},{3,4},{4,1},{5,2},{6,3},{7,0},{8,13},{9,14},{10,... | collective-permute-start | bytes 1179656 | tf_op jit(solution)/shard_map/ppermute | solution.py:479
  209.0 18.6 %collective-permute-start.26 = (bf16[128,1536]{0,1:T(8,128)(2,1)}, bf16[128,1536]{0,1:T(8,128)(2,1)}, u32[]{:S(2)}, u32[]{:S(2)}) collective-permute-start(bf16[128,1536]{0,1:T(8,128)(2,1)} %multiply_convert_fusion), channel_id=1, source_target_pairs={{0,6},{1,7},{2,4},{3,5},{4,2},{5,3},{6,0},{7,1},{8,14},{9,15},{10,... | collective-permute-start | bytes 1179656 | tf_op jit(solution)/shard_map/ppermute | solution.py:479
  310.2 27.2 %collective-permute-start.49 = (bf16[128,1536]{0,1:T(8,128)(2,1)}, bf16[128,1536]{0,1:T(8,128)(2,1)}, u32[]{:S(2)}, u32[]{:S(2)}) collective-permute-start(bf16[128,1536]{0,1:T(8,128)(2,1)} %bitcast.84), channel_id=1, source_target_pairs={{0,1},{1,2},{2,3},{3,0},{4,5},{5,6},{6,7},{7,4},{8,9},{9,10},{10,1... | collective-permute-start | bytes 1179656 | tf_op jit(solution)/shard_map/ppermute | solution.py:479
  312.9 25.1 %collective-permute-start.50 = (bf16[128,1536]{0,1:T(8,128)(2,1)}, bf16[128,1536]{0,1:T(8,128)(2,1)}, u32[]{:S(2)}, u32[]{:S(2)}) collective-permute-start(bf16[128,1536]{0,1:T(8,128)(2,1)} %bitcast.85), channel_id=1, source_target_pairs={{0,2},{1,3},{2,0},{3,1},{4,6},{5,7},{6,4},{7,5},{8,10},{9,11},{10,... | collective-permute-start | bytes 1179656 | tf_op jit(solution)/shard_map/ppermute | solution.py:479
  316.4 28.7 %collective-permute-start.51 = (bf16[128,1536]{0,1:T(8,128)(2,1)}, bf16[128,1536]{0,1:T(8,128)(2,1)}, u32[]{:S(2)}, u32[]{:S(2)}) collective-permute-start(bf16[128,1536]{0,1:T(8,128)(2,1)} %bitcast.342), channel_id=1, source_target_pairs={{0,3},{1,0},{2,1},{3,2},{4,7},{5,4},{6,5},{7,6},{8,11},{9,8},{10,9... | collective-permute-start | bytes 1179656 | tf_op jit(solution)/shard_map/ppermute | solution.py:479
  319.2 26.0 %collective-permute-start.52 = (bf16[128,1536]{0,1:T(8,128)(2,1)}, bf16[128,1536]{0,1:T(8,128)(2,1)}, u32[]{:S(2)}, u32[]{:S(2)}) collective-permute-start(bf16[128,1536]{0,1:T(8,128)(2,1)} %bitcast.341), channel_id=1, source_target_pairs={{0,4},{1,5},{2,6},{3,7},{4,0},{5,1},{6,2},{7,3},{8,12},{9,13},{10,... | collective-permute-start | bytes 1179656 | tf_op jit(solution)/shard_map/ppermute | solution.py:479
  321.2 26.6 %collective-permute-start.53 = (bf16[128,1536]{0,1:T(8,128)(2,1)}, bf16[128,1536]{0,1:T(8,128)(2,1)}, u32[]{:S(2)}, u32[]{:S(2)}) collective-permute-start(bf16[128,1536]{0,1:T(8,128)(2,1)} %bitcast.340), channel_id=1, source_target_pairs={{0,5},{1,6},{2,7},{3,4},{4,1},{5,2},{6,3},{7,0},{8,13},{9,14},{10,... | collective-permute-start | bytes 1179656 | tf_op jit(solution)/shard_map/ppermute | solution.py:479
  338.1 20.3 %collective-permute-start.55 = (bf16[128,1536]{0,1:T(8,128)(2,1)S(1)}, bf16[128,1536]{0,1:T(8,128)(2,1)S(1)}, u32[]{:S(2)}, u32[]{:S(2)}) collective-permute-start(bf16[128,1536]{0,1:T(8,128)(2,1)S(1)} %bitcast.336), channel_id=1, source_target_pairs={{0,7},{1,4},{2,5},{3,6},{4,3},{5,0},{6,1},{7,2},{8,15},{9,12},{10,... | collective-permute-start | bytes 1179656 | tf_op jit(solution)/shard_map/ppermute | solution.py:479
  345.1 19.5 %collective-permute-start.77 = (bf16[32,1024]{1,0:T(8,128)(2,1)S(1)}, bf16[32,1024]{1,0:T(8,128)(2,1)S(1)}, u32[]{:S(2)}, u32[]{:S(2)}) collective-permute-start(bf16[32,1024]{1,0:T(8,128)(2,1)S(1)} %get-tuple-element.196), channel_id=1, source_target_pairs={{0,1},{1,2},{2,3},{3,0},{4,5},{5,6},{6,7},{7,4},{8,9},{9,10},{10,1... | collective-permute-start | bytes 196616 | tf_op jit(solution)/shard_map/ppermute | solution.py:479
  345.3 23.8 %collective-permute-start.78 = (bf16[32,1024]{1,0:T(8,128)(2,1)S(1)}, bf16[32,1024]{1,0:T(8,128)(2,1)S(1)}, u32[]{:S(2)}, u32[]{:S(2)}) collective-permute-start(bf16[32,1024]{1,0:T(8,128)(2,1)S(1)} %get-tuple-element.202), channel_id=1, source_target_pairs={{0,2},{1,3},{2,0},{3,1},{4,6},{5,7},{6,4},{7,5},{8,10},{9,11},{10,... | collective-permute-start | bytes 196616 | tf_op jit(solution)/shard_map/ppermute | solution.py:479
  347.8 22.4 %collective-permute-start.79 = (bf16[32,1024]{1,0:T(8,128)(2,1)S(1)}, bf16[32,1024]{1,0:T(8,128)(2,1)S(1)}, u32[]{:S(2)}, u32[]{:S(2)}) collective-permute-start(bf16[32,1024]{1,0:T(8,128)(2,1)S(1)} %get-tuple-element.201), channel_id=1, source_target_pairs={{0,3},{1,0},{2,1},{3,2},{4,7},{5,4},{6,5},{7,6},{8,11},{9,8},{10,9... | collective-permute-start | bytes 196616 | tf_op jit(solution)/shard_map/ppermute | solution.py:479
  350.6 24.5 %collective-permute-start.80 = (bf16[32,1024]{1,0:T(8,128)(2,1)S(1)}, bf16[32,1024]{1,0:T(8,128)(2,1)S(1)}, u32[]{:S(2)}, u32[]{:S(2)}) collective-permute-start(bf16[32,1024]{1,0:T(8,128)(2,1)S(1)} %get-tuple-element.200), channel_id=1, source_target_pairs={{0,4},{1,5},{2,6},{3,7},{4,0},{5,1},{6,2},{7,3},{8,12},{9,13},{10,... | collective-permute-start | bytes 196616 | tf_op jit(solution)/shard_map/ppermute | solution.py:479
  363.9 18.8 %collective-permute-start.56 = (bf16[128,1664]{0,1:T(8,128)(2,1)}, bf16[128,1664]{0,1:T(8,128)(2,1)S(1)}, u32[]{:S(2)}, u32[]{:S(2)}) collective-permute-start(bf16[128,1664]{0,1:T(8,128)(2,1)} %get-tuple-element.203), channel_id=1, source_target_pairs={{0,1},{1,2},{2,3},{3,0},{4,5},{5,6},{6,7},{7,4},{8,9},{9,10},{10,1... | collective-permute-start | bytes 1277960 | tf_op jit(solution)/shard_map/ppermute | solution.py:479
  364.6 22.4 %collective-permute-start.57 = (bf16[128,1664]{0,1:T(8,128)(2,1)}, bf16[128,1664]{0,1:T(8,128)(2,1)S(1)}, u32[]{:S(2)}, u32[]{:S(2)}) collective-permute-start(bf16[128,1664]{0,1:T(8,128)(2,1)} %get-tuple-element.203), channel_id=1, source_target_pairs={{0,2},{1,3},{2,0},{3,1},{4,6},{5,7},{6,4},{7,5},{8,10},{9,11},{10,... | collective-permute-start | bytes 1277960 | tf_op jit(solution)/shard_map/ppermute | solution.py:479
  377.7 16.9 %collective-permute-start.58 = (bf16[128,1664]{0,1:T(8,128)(2,1)}, bf16[128,1664]{0,1:T(8,128)(2,1)}, u32[]{:S(2)}, u32[]{:S(2)}) collective-permute-start(bf16[128,1664]{0,1:T(8,128)(2,1)} %get-tuple-element.203), channel_id=1, source_target_pairs={{0,3},{1,0},{2,1},{3,2},{4,7},{5,4},{6,5},{7,6},{8,11},{9,8},{10,9... | collective-permute-start | bytes 1277960 | tf_op jit(solution)/shard_map/ppermute | solution.py:479
  377.7 18.1 %collective-permute-start.59 = (bf16[128,1664]{0,1:T(8,128)(2,1)}, bf16[128,1664]{0,1:T(8,128)(2,1)}, u32[]{:S(2)}, u32[]{:S(2)}) collective-permute-start(bf16[128,1664]{0,1:T(8,128)(2,1)} %get-tuple-element.203), channel_id=1, source_target_pairs={{0,4},{1,5},{2,6},{3,7},{4,0},{5,1},{6,2},{7,3},{8,12},{9,13},{10,... | collective-permute-start | bytes 1277960 | tf_op jit(solution)/shard_map/ppermute | solution.py:479
  449.0 18.7 %collective-permute-start.71 = (bf16[32,1024]{1,0:T(8,128)(2,1)S(1)}, bf16[32,1024]{1,0:T(8,128)(2,1)}, u32[]{:S(2)}, u32[]{:S(2)}) collective-permute-start(bf16[32,1024]{1,0:T(8,128)(2,1)S(1)} %get-tuple-element.195), channel_id=1, source_target_pairs={{0,2},{1,3},{2,0},{3,1},{4,6},{5,7},{6,4},{7,5},{8,10},{9,11},{10,... | collective-permute-start | bytes 196616 | tf_op jit(solution)/shard_map/ppermute | solution.py:479
  469.5 325.0 %all-reduce.15.cloned.1.call-start = ((), (), s32[]{:S(2)}) async-start(), calls=%async_computation.1 | async-start | bytes 14548992 | tf_op jit(solution)/shard_map/psum | solution.py:660
  518.6 17.6 %collective-permute-start.63 = (bf16[128,1536]{0,1:T(8,128)(2,1)}, bf16[128,1536]{0,1:T(8,128)(2,1)}, u32[]{:S(2)}, u32[]{:S(2)}) collective-permute-start(bf16[128,1536]{0,1:T(8,128)(2,1)} %bitcast.339), channel_id=1, source_target_pairs={{0,1},{1,2},{2,3},{3,0},{4,5},{5,6},{6,7},{7,4},{8,9},{9,10},{10,1... | collective-permute-start | bytes 1179656 | tf_op jit(solution)/shard_map/ppermute | solution.py:479
  520.9 21.4 %collective-permute-start.64 = (bf16[128,1536]{0,1:T(8,128)(2,1)}, bf16[128,1536]{0,1:T(8,128)(2,1)}, u32[]{:S(2)}, u32[]{:S(2)}) collective-permute-start(bf16[128,1536]{0,1:T(8,128)(2,1)} %bitcast.337), channel_id=1, source_target_pairs={{0,2},{1,3},{2,0},{3,1},{4,6},{5,7},{6,4},{7,5},{8,10},{9,11},{10,... | collective-permute-start | bytes 1179656 | tf_op jit(solution)/shard_map/ppermute | solution.py:479
  525.0 122.6 %collective-permute-start.65 = (bf16[128,1536]{0,1:T(8,128)(2,1)}, bf16[128,1536]{0,1:T(8,128)(2,1)}, u32[]{:S(2)}, u32[]{:S(2)}) collective-permute-start(bf16[128,1536]{0,1:T(8,128)(2,1)} %bitcast.333), channel_id=1, source_target_pairs={{0,3},{1,0},{2,1},{3,2},{4,7},{5,4},{6,5},{7,6},{8,11},{9,8},{10,9... | collective-permute-start | bytes 1179656 | tf_op jit(solution)/shard_map/ppermute | solution.py:479
  525.9 121.7 %collective-permute-start.66 = (bf16[128,1536]{0,1:T(8,128)(2,1)}, bf16[128,1536]{0,1:T(8,128)(2,1)}, u32[]{:S(2)}, u32[]{:S(2)}) collective-permute-start(bf16[128,1536]{0,1:T(8,128)(2,1)} %bitcast.106), channel_id=1, source_target_pairs={{0,4},{1,5},{2,6},{3,7},{4,0},{5,1},{6,2},{7,3},{8,12},{9,13},{10,... | collective-permute-start | bytes 1179656 | tf_op jit(solution)/shard_map/ppermute | solution.py:479
  528.0 119.6 %collective-permute-start.67 = (bf16[128,1536]{0,1:T(8,128)(2,1)}, bf16[128,1536]{0,1:T(8,128)(2,1)}, u32[]{:S(2)}, u32[]{:S(2)}) collective-permute-start(bf16[128,1536]{0,1:T(8,128)(2,1)} %bitcast.107), channel_id=1, source_target_pairs={{0,5},{1,6},{2,7},{3,4},{4,1},{5,2},{6,3},{7,0},{8,13},{9,14},{10,... | collective-permute-start | bytes 1179656 | tf_op jit(solution)/shard_map/ppermute | solution.py:479
  536.2 111.4 %collective-permute-start.68 = (bf16[128,1536]{0,1:T(8,128)(2,1)}, bf16[128,1536]{0,1:T(8,128)(2,1)}, u32[]{:S(2)}, u32[]{:S(2)}) collective-permute-start(bf16[128,1536]{0,1:T(8,128)(2,1)} %bitcast.335), channel_id=1, source_target_pairs={{0,6},{1,7},{2,4},{3,5},{4,2},{5,3},{6,0},{7,1},{8,14},{9,15},{10,... | collective-permute-start | bytes 1179656 | tf_op jit(solution)/shard_map/ppermute | solution.py:479
  542.4 105.2 %collective-permute-start.69 = (bf16[128,1536]{0,1:T(8,128)(2,1)}, bf16[128,1536]{0,1:T(8,128)(2,1)}, u32[]{:S(2)}, u32[]{:S(2)}) collective-permute-start(bf16[128,1536]{0,1:T(8,128)(2,1)} %bitcast.334), channel_id=1, source_target_pairs={{0,7},{1,4},{2,5},{3,6},{4,3},{5,0},{6,1},{7,2},{8,15},{9,12},{10,... | collective-permute-start | bytes 1179656 | tf_op jit(solution)/shard_map/ppermute | solution.py:479
  (110 other events, 1932.3 us)
Sparse Core Ops, SparseCore 0:
  469.6 138.7 all-reduce.12
  613.0 181.4 all-reduce.14

commit v2 on v1

v2 whole, which is shorter than its diff:
```python
import functools

import jax
import jax.numpy as jnp
from jax import lax
from jax.experimental import pallas as pl
from jax.experimental.pallas import tpu as pltpu
from jax.sharding import PartitionSpec as P

SPAN = 256
EPS = 1e-05
LANES = 128
VMEM_BYTES = 56 * 1024 * 1024

f32 = jnp.float32
bf16 = jnp.bfloat16
highest = lax.Precision.HIGHEST

ROWS = ((0,), (0,))
COLS = ((1,), (1,))
PLAIN = ((1,), (0,))


def dot(left, right, dims=PLAIN, precision=None):
    return lax.dot_general(
        left, right, (dims, ((), ())), preferred_element_type=f32, precision=precision
    )


def sigmoid(v):
    return 1.0 / (1.0 + jnp.exp(-v))


def softplus(v):
    return jnp.maximum(v, 0.0) + jnp.log1p(jnp.exp(-jnp.abs(v)))


def spread_heads(per_head, channels, head_dim):
    rows = per_head.shape[0]
    per_tile = LANES // head_dim
    lane = lax.broadcasted_iota(jnp.int32, (rows, LANES), 1)
    tiles = []
    for tile in range(channels // LANES):
        out = jnp.broadcast_to(
            per_head[:, tile * per_tile : tile * per_tile + 1], (rows, LANES)
        )
        for sub in range(1, per_tile):
            head = tile * per_tile + sub
            out = jnp.where(
                lane >= sub * head_dim,
                jnp.broadcast_to(per_head[:, head : head + 1], (rows, LANES)),
                out,
            )
        tiles.append(out)
    return jnp.concatenate(tiles, axis=1)


def conv_taps(buf, taps, offset, width):
    out = offset
    for j in range(4):
        out = out + taps[j : j + 1] * buf[pl.ds(5 + j, width), :]
    return out


def decay_matrix(mask, cum_col, cum_row):
    return jnp.exp(jnp.where(mask, cum_col - cum_row, -1e30))


def span_values(dt, head_ref):
    length = dt.shape[0]
    rows = lax.broadcasted_iota(jnp.int32, (length, length), 0)
    cols = lax.broadcasted_iota(jnp.int32, (length, length), 1)
    mask = rows >= cols
    pre = dt + head_ref[0:1, :]
    step = softplus(pre)
    rate = head_ref[1:2, :] * step
    cum = dot(mask.astype(f32), rate, PLAIN, highest)
    return mask, pre, step, rate, cum


def put_half(place_ref, span, half, mine_ref, other_ref, value):
    own = span // half == place_ref[0]

    @pl.when(own)
    def _():
        mine_ref[...] = value

    @pl.when(jnp.logical_not(own))
    def _():
        other_ref[...] = value


def forward_kernel(last_layer, head_dim, place_ref, *refs):
    if last_layer:
        (xn_ref, wz_ref, wx_ref, wbc_ref, wdt_ref, wo_ref, cx_ref, cbc_ref, head_ref, g_ref,
         z_ref, xp_ref, bc_ref, dt_ref, y_ref, hin_ref, mine_ref, other_ref, sums_ref, gg_ref, xbuf, bbuf, hst) = refs
    else:
        (xn_ref, wz_ref, wx_ref, wbc_ref, wdt_ref, wo_ref, cx_ref, cbc_ref, head_ref,
         z_ref, xp_ref, bc_ref, dt_ref, y_ref, hin_ref, mine_ref, other_ref, xbuf, bbuf, hst) = refs
    length = xn_ref.shape[0]
    channels = wz_ref.shape[1]
    state = hst.shape[0]

    @pl.when(pl.program_id(0) == 0)
    def _():
        xbuf[0:8, :] = jnp.zeros((8, channels), f32)
        bbuf[0:8, :] = jnp.zeros((8, 2 * state), f32)
        hst[...] = jnp.zeros_like(hst)

    xn = xn_ref[...]
    z = dot(xn, wz_ref[...])
    z_ref[...] = z
    xp = dot(xn, wx_ref[...])
    xp_ref[...] = xp
    xbuf[8:, :] = xp
    bc = dot(xn, wbc_ref[...], COLS).astype(bf16)
    bc_ref[...] = bc
    bbuf[8:, :] = bc.astype(f32)
    dt = dot(xn, wdt_ref[...], COLS)
    dt_ref[...] = dt

    pre_x = conv_taps(xbuf, cx_ref[0:4, :], cx_ref[4:5, :], length)
    xc = pre_x * sigmoid(pre_x)
    pre_bc = conv_taps(bbuf, cbc_ref[0:4, :], cbc_ref[4:5, :], length)
    bcc = (pre_bc * sigmoid(pre_bc)).astype(bf16)
    xbuf[0:8, :] = xbuf[length : length + 8, :]
    bbuf[0:8, :] = bbuf[length : length + 8, :]
    b_mat = bcc[:, :state]
    c_mat = bcc[:, state:]

    mask, _, step, _, cum = span_values(dt, head_ref)
    cum_t = jnp.transpose(cum)
    scores = dot(c_mat, b_mat, COLS)
    xs = xc * spread_heads(step, channels, head_dim)
    xs_b = xs.astype(bf16)
    lane = lax.broadcasted_iota(jnp.int32, (length, LANES), 1)
    per_tile = LANES // head_dim
    tiles = []
    for tile in range(channels // LANES):
        xs_tile = xs_b[:, tile * LANES : (tile + 1) * LANES]
        out = None
        for sub in range(per_tile):
            head = tile * per_tile + sub
            decay = decay_matrix(mask, cum[:, head : head + 1], cum_t[head : head + 1, :])
            part = dot((scores * decay).astype(bf16), xs_tile)
            out = part if out is None else jnp.where(lane >= sub * head_dim, part, out)
        tiles.append(out)
    hin = hst[...]
    hin_ref[0] = hin
    last = cum[length - 1 : length, :]
    y = jnp.concatenate(tiles, axis=1)
    y = y + dot(c_mat, hin.astype(bf16)) * spread_heads(jnp.exp(cum), channels, head_dim)
    y = y + cx_ref[6:7, :] * xc
    y_ref[...] = y
    tail = spread_heads(jnp.exp(last - cum), channels, head_dim)
    keep = spread_heads(jnp.exp(last), channels, head_dim)
    hst[...] = keep * hin + dot(b_mat, (tail * xs).astype(bf16), ROWS)

    gated = y * (z * sigmoid(z))
    scaled = gated * cx_ref[5:6, :]
    squares = jnp.sum(gated * gated, axis=1, keepdims=True)
    high = squares.astype(bf16).astype(f32)
    extra = jnp.where(lane == 0, high, jnp.where(lane == 1, squares - high, 0.0)).astype(bf16)
    mixed = dot(scaled.astype(bf16), wo_ref[...]).astype(bf16)
    put_half(
        place_ref,
        pl.program_id(0),
        pl.num_programs(0) // 2,
        mine_ref,
        other_ref,
        jnp.concatenate([mixed, extra], axis=1),
    )
    if last_layer:
        gg = dot(g_ref[...], wo_ref[...], COLS)
        gg_ref[...] = gg
        products = jnp.sum(gg * scaled, axis=1, keepdims=True)
        both = jnp.where(lane == 0, squares, jnp.where(lane == 1, products, 0.0))
        sums_ref[...] = jnp.transpose(both)[0:8, :]


def backward_kernel(last_layer, head_dim, inner_all, place_ref, *refs):
    (first_ref, xn_ref, tok_ref, z_ref, xp_ref, xhalo_ref, bc_ref, bchalo_ref, dt_ref, y_ref, hin_ref,
     wz_ref, wx_ref, wbc_ref, wdt_ref, wo_ref, cx_ref, cbc_ref, head_ref, pick_ref,
     go_ref, dz_ref, dx_ref, dbc_ref, ddt_ref, mine_ref, other_ref, acc_ref, accbc_ref, acch_ref, accn_ref,
     xbuf, bbuf, dubuf, dubbuf, dhst) = refs
    length = z_ref.shape[0]
    channels = wz_ref.shape[1]
    state = dhst.shape[0]
    width = wo_ref.shape[1]
    step_id = pl.program_id(0)
    first_span = step_id == pl.num_programs(0) - 1

    @pl.when(step_id == 0)
    def _():
        dubuf[length:, :] = jnp.zeros((8, channels), f32)
        dubbuf[length:, :] = jnp.zeros((8, 2 * state), f32)
        dhst[...] = jnp.zeros_like(dhst)
        accn_ref[...] = jnp.zeros_like(accn_ref)
        acc_ref[...] = jnp.zeros_like(acc_ref)
        accbc_ref[...] = jnp.zeros_like(accbc_ref)
        acch_ref[...] = jnp.zeros_like(acch_ref)

    @pl.when(first_span)
    def _():
        xbuf[0:8, :] = jnp.zeros((8, channels), f32)
        bbuf[0:8, :] = jnp.zeros((8, 2 * state), f32)

    @pl.when(jnp.logical_not(first_span))
    def _():
        xbuf[0:8, :] = xhalo_ref[...]
        bbuf[0:8, :] = bchalo_ref[...].astype(f32)[8:16, :]

    xbuf[8:, :] = xp_ref[...]
    bbuf[8:, :] = bc_ref[...].astype(f32)

    if last_layer:
        gg = first_ref[...]
        tok = jnp.transpose(tok_ref[...])
        rms = lax.rsqrt(tok[:, 0:1] / inner_all + EPS)
        coef = rms * rms * rms * tok[:, 1:2] / inner_all
    else:
        gg = dot(first_ref[:, :width], wo_ref[...], COLS)
        tok = first_ref[:, width:].astype(f32)
        rms = tok[:, 0:1] + tok[:, 1:2]
        coef = tok[:, 2:3] + tok[:, 3:4]
    norm_gate = cx_ref[5:6, :]
    skip = cx_ref[6:7, :]
    z = z_ref[...]
    y = y_ref[...]
    sz = sigmoid(z)
    silu_z = z * sz
    gated = y * silu_z
    rg = rms * gg
    gated_rms = gated * rms
    go_ref[...] = (gated_rms * norm_gate).astype(bf16)
    d_gated = rg * norm_gate - gated * coef
    acc_norm = jnp.sum(rg * gated, axis=0, keepdims=True)
    dz_b = (d_gated * y * (sz * (1.0 + z * (1.0 - sz)))).astype(bf16)
    dz_ref[...] = dz_b
    dy = d_gated * silu_z

    pre_x = conv_taps(xbuf, cx_ref[0:4, :], cx_ref[4:5, :], length)
    sx = sigmoid(pre_x)
    xc = pre_x * sx
    pre_bc = conv_taps(bbuf, cbc_ref[0:4, :], cbc_ref[4:5, :], length)
    sbc = sigmoid(pre_bc)
    bcc = (pre_bc * sbc).astype(bf16)
    b_mat = bcc[:, :state]
    c_mat = bcc[:, state:]
    mask, pre_dt, step, rate, cum = span_values(dt_ref[...], head_ref)
    cum_t = jnp.transpose(cum)
    last = cum[length - 1 : length, :]
    scores = dot(c_mat, b_mat, COLS)
    step_all = spread_heads(step, channels, head_dim)
    xs = xc * step_all
    xs_b = xs.astype(bf16)
    tail = spread_heads(jnp.exp(last - cum), channels, head_dim)
    keep = spread_heads(jnp.exp(last), channels, head_dim)

    hin = hin_ref[0]
    hin_b = hin.astype(bf16)
    dh = dhst[...]
    dh_b = dh.astype(bf16)
    dye = dy * spread_heads(jnp.exp(cum), channels, head_dim)
    dye_b = dye.astype(bf16)
    txs = tail * xs
    txs_b = txs.astype(bf16)
    carried = dot(c_mat, hin_b)
    pulled = dot(b_mat, dh_b)
    d_c = dot(dye_b, hin_b, COLS)
    d_b = dot(txs_b, dh_b, COLS)
    dhst[...] = keep * dh + dot(c_mat, dye_b, ROWS)
    into = txs * pulled
    across = dye * carried - into
    at_last = jnp.sum(into, axis=0, keepdims=True) + keep * jnp.sum(hin * dh, axis=0, keepdims=True)

    dy_b = dy.astype(bf16)
    dy_t = jnp.transpose(dy).astype(bf16)
    lane = lax.broadcasted_iota(jnp.int32, (length, LANES), 1)
    per_tile = LANES // head_dim
    d_scores = jnp.zeros((length, length), f32)
    row_sums = jnp.zeros((length, LANES), f32)
    col_sums = []
    dxs_parts = []
    for head in range(channels // head_dim):
        tile, sub = divmod(head, per_tile)
        dy_tile = dy_b[:, tile * LANES : (tile + 1) * LANES]
        own = (lane >= sub * head_dim) & (lane < (sub + 1) * head_dim)
        dy_head = jnp.where(own, dy_tile, jnp.zeros_like(dy_tile))
        d_m = dot(dy_head, xs_b[:, tile * LANES : (tile + 1) * LANES], COLS)
        decay = decay_matrix(mask, cum[:, head : head + 1], cum_t[head : head + 1, :])
        dxs_parts.append(
            dot(dy_t[head * head_dim : (head + 1) * head_dim, :], (scores * decay).astype(bf16))
        )
        d_m = d_m * decay
        d_scores = d_scores + d_m
        pairs = d_m * scores
        row_sums = jnp.where(lane == head, jnp.sum(pairs, axis=1, keepdims=True), row_sums)
        col_sums.append(jnp.sum(pairs, axis=0, keepdims=True))
    heads = len(col_sums)
    col_sums = jnp.concatenate(col_sums + [jnp.zeros((LANES - heads, length), f32)], axis=0)
    dxs = jnp.transpose(jnp.concatenate(dxs_parts, axis=0)) + tail * pulled
    pick = pick_ref[...]
    d_cum = row_sums - jnp.transpose(col_sums) + dot(across, pick, PLAIN, highest)
    at_last = dot(jnp.broadcast_to(at_last, (8, channels)), pick, PLAIN, highest)[0:1, :]
    d_rate = dot(mask.astype(f32), d_cum, ROWS, highest) + at_last
    d_step = d_rate * head_ref[1:2, :] + dot(dxs * xc, pick, PLAIN, highest)
    d_dt = d_step * sigmoid(pre_dt)
    acch_ref[0:1, :] += jnp.sum(d_dt, axis=0, keepdims=True)
    acch_ref[1:2, :] += jnp.sum(d_rate * rate, axis=0, keepdims=True)
    dt_b = d_dt.astype(bf16)
    ddt_ref[...] = dt_b
    ds_b = d_scores.astype(bf16)
    d_c = d_c + dot(ds_b, b_mat)
    d_b = d_b + dot(ds_b, c_mat, ROWS)
    d_xc = dxs * step_all + skip * dy
    acc_skip = jnp.sum(dy * xc, axis=0, keepdims=True)

    d_u = d_xc * (sx * (1.0 + pre_x * (1.0 - sx)))
    d_ub = jnp.concatenate([d_b, d_c], axis=1) * (sbc * (1.0 + pre_bc * (1.0 - sbc)))
    dubuf[0:length, :] = d_u
    dubbuf[0:length, :] = d_ub
    d_x = jnp.zeros_like(d_u)
    d_bc = jnp.zeros_like(d_ub)
    acc_rows = []
    accbc_rows = []
    for j in range(4):
        d_x = d_x + cx_ref[j : j + 1, :] * dubuf[pl.ds(3 - j, length), :]
        d_bc = d_bc + cbc_ref[j : j + 1, :] * dubbuf[pl.ds(3 - j, length), :]
        acc_rows.append(jnp.sum(d_u * xbuf[pl.ds(5 + j, length), :], axis=0, keepdims=True))
        accbc_rows.append(jnp.sum(d_ub * bbuf[pl.ds(5 + j, length), :], axis=0, keepdims=True))
    dubuf[length:, :] = d_u[0:8, :]
    dubbuf[length:, :] = d_ub[0:8, :]
    zero = jnp.zeros((1, channels), f32)
    acc_ref[...] += jnp.concatenate(
        acc_rows + [jnp.sum(d_u, axis=0, keepdims=True), acc_norm, acc_skip, zero], axis=0
    )
    zero = jnp.zeros((3, d_ub.shape[1]), f32)
    accbc_ref[...] += jnp.concatenate(
        accbc_rows + [jnp.sum(d_ub, axis=0, keepdims=True), zero], axis=0
    )
    dx_b = d_x.astype(bf16)
    dbc_b = d_bc.astype(bf16)
    dx_ref[...] = dx_b
    dbc_ref[...] = jnp.transpose(d_bc).astype(bf16)
    total = dot(dz_b, wz_ref[...], COLS) + dot(dx_b, wx_ref[...], COLS)
    total = total + dot(dbc_b, wbc_ref[...]) + dot(dt_b, wdt_ref[...])
    accn_ref[0:1, :] += jnp.sum(total * xn_ref[...].astype(f32), axis=0, keepdims=True)
    put_half(
        place_ref,
        pl.num_programs(0) - 1 - step_id,
        pl.num_programs(0) // 2,
        mine_ref,
        other_ref,
        total.astype(bf16),
    )


def whole(shape):
    zeros = (0,) * len(shape)
    return pl.BlockSpec(shape, lambda i, p: zeros)


def span_rows(columns):
    return pl.BlockSpec((SPAN, columns), lambda i, p: (i, 0))


def half_rows(columns, spans, reverse):
    half = spans // 2

    def block(i, core):
        span = spans - 1 - i if reverse else i
        return jnp.clip(span - half * core, 0, half - 1), 0

    return [
        pl.BlockSpec((SPAN, columns), lambda i, p: block(i, p[0])),
        pl.BlockSpec((SPAN, columns), lambda i, p: block(i, 1 - p[0])),
    ]


def span_call(kernel, name, spans, place, operands, in_specs, shapes, out_specs, scratch):
    return pl.pallas_call(
        kernel,
        grid_spec=pltpu.PrefetchScalarGridSpec(
            num_scalar_prefetch=1,
            grid=(spans,),
            in_specs=in_specs,
            out_specs=out_specs,
            scratch_shapes=scratch,
        ),
        out_shape=shapes,
        compiler_params=pltpu.CompilerParams(
            dimension_semantics=("arbitrary",), vmem_limit_bytes=VMEM_BYTES
        ),
        name=name,
    )(place, *operands)


def run_forward(place, xn, weights, small, state, head_dim, grad_rows=None):
    tokens, width = xn.shape
    channels = weights[0].shape[1]
    spans = tokens // SPAN
    last_layer = grad_rows is not None
    operands = [xn, *weights, *small]
    in_specs = [span_rows(width)] + [whole(v.shape) for v in operands[1:]]
    shapes = [
        jax.ShapeDtypeStruct((tokens, channels), f32),
        jax.ShapeDtypeStruct((tokens, channels), f32),
        jax.ShapeDtypeStruct((tokens, 2 * state), bf16),
        jax.ShapeDtypeStruct((tokens, LANES), f32),
        jax.ShapeDtypeStruct((tokens, channels), f32),
        jax.ShapeDtypeStruct((spans, state, channels), f32),
        jax.ShapeDtypeStruct((tokens // 2, width + LANES), bf16),
        jax.ShapeDtypeStruct((tokens // 2, width + LANES), bf16),
    ]
    out_specs = [span_rows(s.shape[1]) for s in shapes[:5]]
    out_specs.append(pl.BlockSpec((1, state, channels), lambda i, p: (i, 0, 0)))
    out_specs += half_rows(width + LANES, spans, False)
    if last_layer:
        operands.append(grad_rows)
        in_specs.append(span_rows(width))
        shapes += [
            jax.ShapeDtypeStruct((8, tokens), f32),
            jax.ShapeDtypeStruct((tokens, channels), f32),
        ]
        out_specs += [pl.BlockSpec((8, SPAN), lambda i, p: (0, i)), span_rows(channels)]
    scratch = [
        pltpu.VMEM((SPAN + 8, channels), f32),
        pltpu.VMEM((SPAN + 8, 2 * state), f32),
        pltpu.VMEM((state, channels), f32),
    ]
    kernel = functools.partial(forward_kernel, last_layer, head_dim)
    return span_call(
        kernel, "layer_forward", spans, place, operands, in_specs, shapes, out_specs, scratch
    )


def run_backward(place, first, sums, xn, kept, weights, small, pick, head_dim, inner_all):
    z, xp, bc, dt, y, hin = kept
    tokens, channels = z.shape
    state = hin.shape[1]
    width = weights[4].shape[1]
    spans = tokens // SPAN
    last_layer = sums is not None
    if sums is None:
        sums = jnp.zeros((8, tokens), f32)

    def rev(columns):
        return pl.BlockSpec((SPAN, columns), lambda i, p: (spans - 1 - i, 0))

    def rev_cols(rows):
        return pl.BlockSpec((rows, SPAN), lambda i, p: (0, spans - 1 - i))

    def halo(columns, rows):
        per = SPAN // rows
        return pl.BlockSpec(
            (rows, columns), lambda i, p: (jnp.maximum((spans - 1 - i) * per - 1, 0), 0)
        )

    operands = [first, xn, sums, z, xp, xp, bc, bc, dt, y, hin, *weights, *small, pick]
    in_specs = [
        rev(first.shape[1]),
        rev(width),
        rev_cols(8),
        rev(channels),
        rev(channels),
        halo(channels, 8),
        rev(2 * state),
        halo(2 * state, 16),
        rev(LANES),
        rev(channels),
        pl.BlockSpec((1, state, channels), lambda i, p: (spans - 1 - i, 0, 0)),
    ]
    in_specs += [whole(v.shape) for v in operands[len(in_specs) :]]
    shapes = [
        jax.ShapeDtypeStruct((tokens, channels), bf16),
        jax.ShapeDtypeStruct((tokens, channels), bf16),
        jax.ShapeDtypeStruct((tokens, channels), bf16),
        jax.ShapeDtypeStruct((2 * state, tokens), bf16),
        jax.ShapeDtypeStruct((tokens, LANES), bf16),
        jax.ShapeDtypeStruct((tokens // 2, width), bf16),
        jax.ShapeDtypeStruct((tokens // 2, width), bf16),
        jax.ShapeDtypeStruct((8, channels), f32),
        jax.ShapeDtypeStruct((8, 2 * state), f32),
        jax.ShapeDtypeStruct((8, LANES), f32),
        jax.ShapeDtypeStruct((8, width), f32),
    ]
    out_specs = [rev(channels), rev(channels), rev(channels), rev_cols(2 * state), rev(LANES)]
    out_specs += half_rows(width, spans, True)
    out_specs += [whole(s.shape) for s in shapes[7:]]
    scratch = [
        pltpu.VMEM((SPAN + 8, channels), f32),
        pltpu.VMEM((SPAN + 8, 2 * state), f32),
        pltpu.VMEM((SPAN + 8, channels), f32),
        pltpu.VMEM((SPAN + 8, 2 * state), f32),
        pltpu.VMEM((state, channels), f32),
    ]
    kernel = functools.partial(backward_kernel, last_layer, head_dim, inner_all)
    return span_call(
        kernel, "layer_backward", spans, place, operands, in_specs, shapes, out_specs, scratch
    )


SIZES = (4, 2, 2, 2, 4)
NX, NYL, NC, NYH, NZ = SIZES
EVERY = [
    (x, yl, c, yh, z)
    for x in range(NX)
    for yl in range(NYL)
    for c in range(NC)
    for yh in range(NYH)
    for z in range(NZ)
]


def linear(x, yl, c, yh, z):
    return ((((x % NX) * NYL + yl % NYL) * NC + c % NC) * NYH + yh % NYH) * NZ + z % NZ


def send(v, step, only=None):
    pairs = [(linear(*d), linear(*step(*d))) for d in EVERY if only is None or only(*d)]
    return lax.ppermute(v, ("dp", "tensor"), pairs)


def send_z(v, k):
    return send(v, lambda x, yl, c, yh, z: (x, yl, c, yh, z + k))


def send_core(v):
    return send(v, lambda x, yl, c, yh, z: (x, yl, c + 1, yh, z))


def trade(v, k=0):
    return send(v, lambda x, yl, c, yh, z: (x, yl, yh, c, z + k))


def position():
    dp, tensor = lax.axis_index("dp"), lax.axis_index("tensor")
    return dp // (NYL * NC), dp // NC % NYL, dp % NC, tensor // NZ, tensor % NZ


def assemble_kernel(plan, n_pieces, n_out, place_ref, *refs):
    pieces, outs = refs[:n_pieces], refs[n_pieces : n_pieces + n_out]
    core, z = place_ref[0], place_ref[1]
    for piece, other, dz, start, out, per, offset, rows in plan:
        member = (1 - core if other else core) * NZ + lax.rem(z + dz, NZ)
        row = pl.multiple_of(member * per + offset, 16)
        outs[out][pl.ds(row, rows), :] = pieces[piece][start : start + rows, :]


def gather(place, v, parts):
    rows, columns = v.shape
    half = rows // 2
    from_left = send_z(v, 1)
    from_right = send_z(v, -1)
    low = send_z(from_left[:half], 1)
    high = send_z(from_right[half:], -1)
    pieces, plan = [], []
    for piece, dz, first in (
        (v, 0, 0),
        (from_left, NZ - 1, 0),
        (from_right, 1, 0),
        (low, 2, 0),
        (high, 2, half),
    ):
        for other, held in ((False, piece), (True, send_core(piece))):
            base = 0
            for out, per in enumerate(parts):
                begin, end = max(first, base), min(first + held.shape[0], base + per)
                if begin < end:
                    plan.append(
                        (len(pieces), other, dz, begin - first, out, per, begin - base, end - begin)
                    )
                base += per
            pieces.append(held)
    shapes = [jax.ShapeDtypeStruct((NC * NZ * per, columns), v.dtype) for per in parts]
    return pl.pallas_call(
        functools.partial(assemble_kernel, plan, len(pieces), len(parts)),
        grid_spec=pltpu.PrefetchScalarGridSpec(
            num_scalar_prefetch=1,
            grid=(1,),
            in_specs=[whole(p.shape) for p in pieces],
            out_specs=[whole(s.shape) for s in shapes],
        ),
        out_shape=shapes,
        compiler_params=pltpu.CompilerParams(vmem_limit_bytes=VMEM_BYTES),
        name="assemble",
    )(place, *pieces)


def fold_kernel(place_ref, mine_ref, other_ref, *out_refs):
    rows = out_refs[0].shape[0]
    for k, out_ref in enumerate(out_refs):
        at = pl.ds(pl.multiple_of(lax.rem(place_ref[1] + k, NZ) * rows, 16), rows)
        out_ref[...] = (mine_ref[at, :].astype(f32) + other_ref[at, :].astype(f32)).astype(
            out_ref.dtype
        )


def fold(place, mine, other, own_type):
    rows, columns = mine.shape[0] // NZ, mine.shape[1]
    whole_in = pl.BlockSpec(mine.shape, lambda i, p: (0, 0))
    whole_out = pl.BlockSpec((rows, columns), lambda i, p: (0, 0))
    return pl.pallas_call(
        fold_kernel,
        grid_spec=pltpu.PrefetchScalarGridSpec(
            num_scalar_prefetch=1,
            grid=(1,),
            in_specs=[whole_in] * 2,
            out_specs=[whole_out] * NZ,
        ),
        out_shape=[
            jax.ShapeDtypeStruct((rows, columns), own_type if k == 0 else bf16) for k in range(NZ)
        ],
        compiler_params=pltpu.CompilerParams(vmem_limit_bytes=VMEM_BYTES),
        name="fold",
    )(place, mine, other)


def scatter(place, mine, other):
    own, one, two, three = fold(place, mine, send_core(other), f32)
    return own, send_z(one, 1), send_z(two, 2), send_z(three, 3)


def scatter_home(place, mine, other):
    blocks = fold(place, mine, send_core(other), bf16)
    return tuple(trade(block, k) for k, block in enumerate(blocks))


def scatter_rows(v):
    _, _, core, _, z = position()
    cut = v.reshape((NC, NZ, v.shape[0] // (NC * NZ)) + v.shape[1:])
    mine = lax.dynamic_index_in_dim(cut, core, 0, False).astype(f32)
    other = lax.dynamic_index_in_dim(cut, 1 - core, 0, False)
    both = mine + send_core(other).astype(f32)
    total = lax.dynamic_index_in_dim(both, z, 0, False)
    both = both.astype(bf16)
    for k in range(1, NZ):
        block = lax.dynamic_index_in_dim(both, (z + k) % NZ, 0, False)
        total = total + send_z(block, k).astype(f32)
    return total


def sum_members(v):
    both = v + send_core(v)
    total = both
    for k in range(1, NZ):
        total = total + send_z(both, k)
    return total


def reduce_front(v):
    _, _, core, yh, _ = position()
    half = v.shape[0] // 2
    low, high = v[:half], v[half:]

    def away(x, yl, c, yh, z):
        return c != yh

    def home(x, yl, c, yh, z):
        return c == yh

    low_far = send(low, lambda x, yl, c, yh, z: (x, yl, c, yh + 1, z), away)
    high_far = send(high, lambda x, yl, c, yh, z: (x, yl, c + 1, yh + 1, z), away)
    high_near = send(high, lambda x, yl, c, yh, z: (x, yl, c + 1, yh, z), home)
    stays = core == yh
    near = jnp.where(stays, low, high_near).astype(f32)
    far = jnp.where(stays, low_far, high_far).astype(f32)
    return (near + far).astype(bf16)


def reduce_back(half):
    _, _, core, yh, _ = position()
    other = send_core(half)
    stays = core == yh
    return jnp.concatenate([jnp.where(stays, half, other), jnp.where(stays, other, half)], axis=0)


def sum_chips(v):
    x, yl, _, _, _ = position()
    cut = v.reshape((NX, v.shape[0] // NX) + v.shape[1:])
    total = lax.dynamic_index_in_dim(cut, x, 0, False).astype(f32)
    for k in range(1, NX):
        block = lax.dynamic_index_in_dim(cut, (x + k) % NX, 0, False)
        total = total + send(block, lambda x, yl, c, yh, z, k=k: (x + k, yl, c, yh, z)).astype(f32)

    def beside(v):
        return send(v, lambda x, yl, c, yh, z: (x, yl + 1, c, yh, z))

    total = total.astype(bf16)
    total = (total.astype(f32) + beside(total).astype(f32)).astype(bf16)
    out = jnp.zeros(cut.shape, bf16)
    out = lax.dynamic_update_index_in_dim(out, total, x, 0)
    for k in range(1, NX):
        block = send(total, lambda x, yl, c, yh, z, k=k: (x + k, yl, c, yh, z))
        out = lax.dynamic_update_index_in_dim(out, block, (x - k) % NX, 0)
    return out.reshape(v.shape)


def sum_chips_beside(v):
    groups = [[2 * k + c for k in range(NX * NYL)] for c in range(NC)]
    return lax.psum(v, "dp", axis_index_groups=groups)


def row_call(kernel, name, operands, shapes):
    return pl.pallas_call(
        kernel,
        grid=(1,),
        in_specs=[pl.BlockSpec((rows, v.shape[1]), lambda i: (0, 0)) for v, rows in operands],
        out_specs=[pl.BlockSpec(s.shape, lambda i: (0, 0)) for s in shapes],
        out_shape=shapes,
        compiler_params=pltpu.CompilerParams(vmem_limit_bytes=VMEM_BYTES),
        name=name,
    )(*[v for v, _ in operands])


def inverse_rms(v):
    return lax.rsqrt(jnp.mean(v * v, axis=-1, keepdims=True) + EPS)


def first_kernel(packed_ref, gain_ref, out_ref):
    rows = 128
    v = packed_ref[0:rows, :].astype(f32)
    out_ref[0:rows, :] = (v * inverse_rms(v) * gain_ref[...]).astype(bf16)
    out_ref[rows:, :] = packed_ref[rows : out_ref.shape[0], :]


def add_terms(own_ref, a_ref, b_ref, c_ref):
    total = own_ref[...].astype(f32) + a_ref[...].astype(f32)
    return total + (b_ref[...].astype(f32) + c_ref[...].astype(f32))


def unscaled_output(inner_all, terms, width):
    total = add_terms(*terms)
    squares = total[:, width : width + 1] + total[:, width + 1 : width + 2]
    gate_rms = lax.rsqrt(squares / inner_all + EPS)
    return gate_rms, total[:, :width] * gate_rms


def middle_kernel(inner_all, own_ref, a_ref, b_ref, c_ref, res_ref, gain_ref, res1_ref, mixed_ref, rms_ref, normed_ref):
    width = res_ref.shape[1]
    gate_rms, mixed = unscaled_output(inner_all, (own_ref, a_ref, b_ref, c_ref), width)
    res = res_ref[...].astype(f32) + mixed
    res1_ref[...] = res
    mixed_ref[...] = mixed
    rms_ref[...] = jnp.broadcast_to(gate_rms, rms_ref.shape)
    normed_ref[...] = (res * inverse_rms(res) * gain_ref[...]).astype(bf16)


def last_kernel(inner_all, own_ref, a_ref, b_ref, c_ref, res_ref, out_ref):
    _, mixed = unscaled_output(inner_all, (own_ref, a_ref, b_ref, c_ref), res_ref.shape[1])
    out_ref[...] = res_ref[...] + mixed


def input_gradient(grad_normed, res, d_res, gain):
    inv = inverse_rms(res)
    scaled = grad_normed * gain
    dots = jnp.sum(scaled * res, axis=-1, keepdims=True) / res.shape[1]
    return d_res + inv * scaled - res * (inv * inv * inv) * dots


def between_kernel(inner_all, own_ref, a_ref, b_ref, c_ref, res_ref, dres_ref, gain_ref, mixed_ref, rms_ref, out_ref, sent_ref):
    width = res_ref.shape[1]
    grad_normed = add_terms(own_ref, a_ref, b_ref, c_ref)
    d_res = input_gradient(grad_normed, res_ref[...], dres_ref[...].astype(f32), gain_ref[...])
    out_ref[...] = d_res
    g_mixed = d_res.astype(bf16)
    sent_ref[:, :width] = g_mixed
    gate_rms = rms_ref[:, 0:1]
    products = jnp.sum(g_mixed.astype(f32) * mixed_ref[...], axis=-1, keepdims=True)
    coef = gate_rms * gate_rms * products / inner_all
    lane = lax.broadcasted_iota(jnp.int32, rms_ref.shape, 1)
    rms_high = gate_rms.astype(bf16).astype(f32)
    coef_high = coef.astype(bf16).astype(f32)
    extra = jnp.where(lane == 0, rms_high, jnp.where(lane == 1, gate_rms - rms_high, 0.0))
    extra = jnp.where(lane == 2, coef_high, jnp.where(lane == 3, coef - coef_high, extra))
    sent_ref[:, width:] = extra.astype(bf16)


def end_kernel(own_ref, a_ref, b_ref, c_ref, res_ref, dres_ref, gain_ref, out_ref):
    grad_normed = add_terms(own_ref, a_ref, b_ref, c_ref)
    out_ref[...] = input_gradient(
        grad_normed, res_ref[...].astype(f32), dres_ref[...], gain_ref[...]
    )


def after(v, *others):
    return lax.optimization_barrier((v, *others))[0]


def pad_to(v, rows, lanes):
    return jnp.pad(v, ((0, rows - v.shape[0]), (0, lanes - v.shape[1])))


def local(
    hidden_in,
    grad_out,
    norm_in,
    w_z,
    w_x,
    w_bc,
    w_dt,
    conv_x,
    conv_x_bias,
    conv_bc,
    conv_bc_bias,
    dt_bias,
    a_log,
    skip,
    norm_gate,
    w_out,
):
    layers, width, channels = w_z.shape
    heads = w_dt.shape[2]
    head_dim = channels // heads
    both = conv_bc.shape[2]
    state = both // 2
    members = NC * NZ
    inner_all = channels * members
    rows = hidden_in.shape[1]
    bc_rows = both // members
    _, _, core, _, z = position()
    place = jnp.stack([core, z]).astype(jnp.int32)

    bc_t = jnp.swapaxes(w_bc, 1, 2)
    dt_t = jnp.pad(jnp.swapaxes(w_dt, 1, 2), ((0, 0), (0, 8 - heads), (0, 0)))
    packed = jnp.concatenate([hidden_in[0], bc_t[0], dt_t.reshape(layers * 8, width)], axis=0)
    packed = trade(packed)
    per_channel = jnp.concatenate(
        [conv_x, conv_x_bias[:, None], norm_gate[:, None], jnp.repeat(skip, head_dim, axis=1)[:, None]],
        axis=1,
    )
    per_channel = jnp.pad(per_channel, ((0, 0), (0, 1), (0, 0)))
    per_head = jnp.stack([dt_bias, -jnp.exp(a_log)], axis=1)
    per_head = jnp.pad(per_head, ((0, 0), (0, 6), (0, LANES - heads)))
    little = jnp.concatenate([per_channel, per_head], axis=2).reshape(layers * 8, channels + LANES)
    little = trade(little).reshape(layers, 8, channels + LANES)
    wz0 = trade(after(w_z[0], packed))
    wx0 = trade(after(w_x[0], packed))
    grads = trade(after(jnp.concatenate([grad_out[0], bc_t[1]], axis=0), wz0, wx0))
    wo0 = trade(after(w_out[0], wz0, wx0))
    wz1 = trade(after(w_z[1], wo0))
    wx1 = trade(after(w_x[1], wo0))
    wo1 = trade(after(w_out[1], wz1, wx1))

    [sent] = row_call(
        first_kernel,
        "first_norm",
        [(packed, packed.shape[0]), (norm_in[0:1], 1)],
        [jax.ShapeDtypeStruct((rows + bc_rows, width), bf16)],
    )
    xn0, wbc0 = gather(place, sent, (rows, bc_rows))
    wdt = [pad_to(packed[rows + bc_rows + 8 * l : rows + bc_rows + 8 * (l + 1)], LANES, width) for l in range(layers)]
    smalls = []
    for layer in range(layers):
        cbc = jnp.concatenate([conv_bc[layer], conv_bc_bias[layer][None], jnp.zeros((3, both), f32)], axis=0)
        smalls.append((little[layer, :, :channels], cbc, little[layer, :, channels:]))
    channel_head = jnp.arange(channels) // head_dim
    pick = (channel_head[:, None] == jnp.arange(LANES)[None, :]).astype(f32)
    weights0 = (wz0, wx0, wbc0, wdt[0], wo0)

    out0 = run_forward(place, xn0, weights0, smalls[0], state, head_dim)
    grad_rows1, wbc1 = gather(place, grads, (rows, bc_rows))
    weights1 = (wz1, wx1, wbc1, wdt[1], wo1)
    terms = scatter(place, out0[6], out0[7])
    full = jax.ShapeDtypeStruct((rows, width), f32)
    res1, mixed0, rms0, normed1 = row_call(
        functools.partial(middle_kernel, inner_all),
        "middle_norm",
        [(v, rows) for v in terms] + [(packed, rows), (norm_in[1:2], 1)],
        [full, full, jax.ShapeDtypeStruct((rows, LANES), f32), jax.ShapeDtypeStruct((rows, width), bf16)],
    )
    [xn1] = gather(place, normed1, (rows,))
    out1 = run_forward(place, xn1, weights1, smalls[1], state, head_dim, grad_rows1)
    sums = sum_members(out1[8])

    back1 = run_backward(
        place, out1[9], sums, xn1, out1[:6], weights1, smalls[1], pick, head_dim, inner_all
    )
    terms = scatter(place, back1[5], back1[6])
    d_res1, sent = row_call(
        functools.partial(between_kernel, inner_all),
        "between_layers",
        [(v, rows) for v in terms]
        + [(res1, rows), (grads, rows), (norm_in[1:2], 1), (mixed0, rows), (rms0, rows)],
        [full, jax.ShapeDtypeStruct((rows, width + LANES), bf16)],
    )
    [first0] = gather(place, sent, (rows,))

    terms = scatter(place, out1[6], out1[7])
    [hidden_out] = row_call(
        functools.partial(last_kernel, inner_all),
        "last_output",
        [(v, rows) for v in terms] + [(res1, rows)],
        [full],
    )
    hidden_out = trade(hidden_out)

    def weight_grads(back, xn, grad_rows):
        gate_out, dz, dx, dbc, ddt = back[:5]
        wide = jnp.concatenate([dot(xn, dz, ROWS).astype(bf16), dot(xn, dx, ROWS).astype(bf16)], axis=0)
        bc_sum = scatter_rows(dbc).astype(bf16)
        narrow = jnp.concatenate([dot(bc_sum, xn), dot(ddt, xn, ROWS)[:8]], axis=0)
        return wide, narrow, dot(gate_out, grad_rows, ROWS).astype(bf16)

    wide1, narrow1, tall1 = weight_grads(back1, xn1, grad_rows1)
    wide1 = reduce_front(wide1)
    tall1 = reduce_front(tall1)
    wide1, tall1 = sum_chips_beside((wide1, tall1))
    wide1, tall1 = reduce_back(wide1), reduce_back(tall1)

    d_res1 = trade(d_res1)
    back0 = run_backward(
        place, first0, None, xn0, out0[:6], weights0, smalls[0], pick, head_dim, inner_all
    )
    terms = scatter_home(place, back0[5], back0[6])
    [grad_in] = row_call(
        end_kernel,
        "input_gradient",
        [(v, rows) for v in terms] + [(hidden_in[0], rows), (d_res1, rows), (norm_in[0:1], 1)],
        [full],
    )
    wide0, narrow0, tall0 = weight_grads(back0, xn0, first0[:, :width])
    wide0 = reduce_back(sum_chips(reduce_front(wide0)))
    tall0 = reduce_back(sum_chips(reduce_front(tall0)))

    shared = jnp.concatenate(
        [back0[10][0:1], back1[10][0:1]]
        + [pad_to(v[8][0:5].reshape(1, 5 * both), 1, width) for v in (back0, back1)],
        axis=0,
    )
    shared = sum_members(shared)
    per_shard = [back0[7].reshape(-1, width), back1[7].reshape(-1, width)]
    per_shard += [pad_to(v[9][0:2].reshape(1, 2 * LANES), 1, width) for v in (back0, back1)]
    misc = jnp.concatenate([narrow0, narrow1, shared] + per_shard, axis=0)
    misc_rows = misc.shape[0]
    misc = pad_to(misc, 128, width).astype(bf16)
    misc = reduce_back(sum_chips(reduce_front(misc))).astype(f32)[:misc_rows]

    at = 0
    parts = []
    for count in (bc_rows, 8, bc_rows, 8, 1, 1, 1, 1, 2, 2, 1, 1):
        parts.append(misc[at : at + count])
        at += count
    g_wbc = jnp.stack([parts[0].T, parts[2].T])
    g_wdt = jnp.stack([parts[1][:heads].T, parts[3][:heads].T])
    g_norm_in = jnp.concatenate([parts[4], parts[5]], axis=0) / norm_in
    g_bc = jnp.concatenate([parts[6], parts[7]], axis=0)[:, : 5 * both].reshape(layers, 5, both)
    g_x = jnp.stack([parts[8].reshape(8, channels), parts[9].reshape(8, channels)])
    g_head = jnp.concatenate([parts[10], parts[11]], axis=0)[:, : 2 * LANES].reshape(layers, 2, LANES)[:, :, :heads]
    wide = jnp.stack([wide0, wide1]).astype(f32)
    return (
        hidden_out[None],
        grad_in[None],
        g_norm_in,
        wide[:, :width],
        wide[:, width:],
        g_wbc,
        g_wdt,
        g_x[:, 0:4],
        g_x[:, 4],
        g_bc[:, 0:4],
        g_bc[:, 4],
        g_head[:, 0],
        g_head[:, 1],
        jnp.sum(g_x[:, 6].reshape(layers, heads, head_dim), axis=2),
        g_x[:, 5],
        jnp.stack([tall0, tall1]).astype(f32),
    )


def solution(mesh):
    specs_in = (
        P("dp", "tensor", None),
        P("dp", "tensor", None),
        P(),
        P(None, None, "tensor"),
        P(None, None, "tensor"),
        P(None, None, "tensor"),
        P(None, None, "tensor"),
        P(None, None, "tensor"),
        P(None, "tensor"),
        P(),
        P(),
        P(None, "tensor"),
        P(None, "tensor"),
        P(None, "tensor"),
        P(None, "tensor"),
        P(None, "tensor", None),
    )
    specs_out = (
        P("dp", "tensor", None),
        P("dp", "tensor", None),
        P(),
        P(None, None, "tensor"),
        P(None, None, "tensor"),
        P(None, None, "tensor"),
        P(None, None, "tensor"),
        P(None, None, "tensor"),
        P(None, "tensor"),
        P(),
        P(),
        P(None, "tensor"),
        P(None, "tensor"),
        P(None, "tensor"),
        P(None, "tensor"),
        P(None, "tensor", None),
    )
    return jax.shard_map(
        local, mesh=mesh, in_specs=specs_in, out_specs=specs_out, check_vma=False
    )
```

time: 824 us -> 654 us (0.79)
  the two profiles are of different devices: /device:TPU:1 before, /device:TPU:8 now
where the time goes in v2:
time: 654 us; the launch traced here: 642 us
  starting transfers between devices  255 us (39%)
  Pallas kernels  156 us (24%)
  waiting for transfers between devices  97.9 us (15%)
  local copies, waits for them, and re-layouts  56.8 us (9%)
  other arithmetic  36.8 us (6%)
  matrix products  22.7 us (3%)
  between operations  16 us (2%)
    ppermute x121, starting transfers between devices, send(): return lax.ppermute(v, ('dp', 'tensor'), pairs)  255 us
    pallas_call x4, Pallas kernels, span_call(): pl.pallas_call(kernel, grid_spec=pltpu.PrefetchScalarGridSpec(num_scalar_...  106 us
    ppermute x121, waiting for transfers between devices, send(): return lax.ppermute(v, ('dp', 'tensor'), pairs)  97.9 us
    dot_general x10, matrix products, dot(): lax.dot_general(left, right, (dims, ((), ())), preferred_element_type=f32...  22.7 us
    pallas_call x4, Pallas kernels, gather(): pl.pallas_call(functools.partial(assemble_kernel, plan, len(pieces), len(...  18.7 us
    unnamed x210, local copies, waits for them, and re-layouts  17 us
    pallas_call x4, Pallas kernels, fold(): pl.pallas_call(fold_kernel, grid_spec=pltpu.PrefetchScalarGridSpec(num_sc...  16.4 us
    pallas_call x5, Pallas kernels, row_call(): pl.pallas_call(kernel, grid=(1,), in_specs=[pl.BlockSpec((rows, v.shape[1...  15.4 us
  transfers between devices with their start and end apart: 122, of which 30 were waited for; matrix products, arithmetic and copies ran while one was open for 15% of the time, Pallas kernels for 13%

profile of v2, /device:TPU:8, one launch (start us, length us, event | category | flops | bytes accessed | tf_op | source)
XLA Modules:
  0.0 641.8 jit_solution(2414990565897344675)
XLA Ops:
  13.7 3.4 slice_bitcast_fusion.2
  29.6 12.7 %collective-permute-start.1 = (bf16[160,1536]{1,0:T(8,128)(2,1)}, bf16[160,1536]{1,0:T(8,128)(2,1)S(1)}, u32[]{:S(2)}, u32[]{:S(2)}) collective-permute-start(bf16[160,1536]{1,0:T(8,128)(2,1)} %first_norm.1.refs_0_), channel_id=1, source_target_pairs={{0,8},{1,9},{2,10},{3,11},{4,12},{5,13},{6,14},{7,15},{8,0},{9,1},... | collective-permute-start | bytes 1474568 | tf_op jit(solution)/shard_map/ppermute | solution.py:522
  50.0 16.1 %collective-permute-start.3 = (bf16[160,1536]{1,0:T(8,128)(2,1)S(1)}, bf16[160,1536]{1,0:T(8,128)(2,1)S(1)}, u32[]{:S(2)}, u32[]{:S(2)}) collective-permute-start(bf16[160,1536]{1,0:T(8,128)(2,1)S(1)} %collective-permute-done.2.refs_2_), channel_id=1, source_target_pairs={{0,8},{1,9},{2,10},{3,11},{4,12},{5,13},{6,14},{7,15},{8,0},{9,1},... | collective-permute-start | bytes 1474568 | tf_op jit(solution)/shard_map/ppermute | solution.py:522
  71.5 4.9 assemble.4
  77.5 20.7 %layer_forward.2 = (f32[1024,384]{1,0:T(8,128)}, f32[1024,384]{1,0:T(8,128)}, bf16[1024,256]{1,0:T(8,128)(2,1)}, f32[1024,128]{1,0:T(8,128)}, f32[1024,384]{1,0:...) custom-call(s32[2]{0:T(128)} %pad_add_fusion.place_ref, ...), custom_call_target="tpu_custom_call" | custom-call | tf_op jit(solution)/shard_map/layer_forward/pallas_call | solution.py:382
  105.5 4.1 fold.4
  114.4 20.8 %collective-permute-start.30 = (bf16[160,1536]{1,0:T(8,128)(2,1)S(1)}, bf16[160,1536]{1,0:T(8,128)(2,1)S(1)}, u32[]{:S(2)}, u32[]{:S(2)}) collective-permute-start(bf16[160,1536]{1,0:T(8,128)(2,1)S(1)} %collective-permute-done.29.refs_0_.dres_ref), channel_id=1, source_target_pairs={{0,8},{1,9},{2,10},{3,11},{4,12},{5,13},{6,14},{7,15},{8,0},{9,1},... | collective-permute-start | bytes 1474568 | tf_op jit(solution)/shard_map/ppermute | solution.py:522
  142.2 3.3 middle_norm.1
  149.9 10.4 %collective-permute-start.34 = (bf16[160,1536]{1,0:T(8,128)(2,1)}, bf16[160,1536]{1,0:T(8,128)(2,1)S(1)}, u32[]{:S(2)}, u32[]{:S(2)}) collective-permute-start(bf16[160,1536]{1,0:T(8,128)(2,1)} %collective-permute-done.33.refs_4_), channel_id=1, source_target_pairs={{0,8},{1,9},{2,10},{3,11},{4,12},{5,13},{6,14},{7,15},{8,0},{9,1},... | collective-permute-start | bytes 1474568 | tf_op jit(solution)/shard_map/ppermute | solution.py:522
  160.5 4.3 collective-permute-start.36
  169.2 4.2 collective-permute-done.23.refs_6_
  174.8 4.9 assemble.6
  181.4 4.4 assemble.5.refs_0_.refs_1_
  186.8 23.3 %layer_forward.3 = (f32[1024,384]{1,0:T(8,128)}, f32[1024,384]{1,0:T(8,128)}, bf16[1024,256]{1,0:T(8,128)(2,1)}, f32[1024,128]{1,0:T(8,128)}, f32[1024,384]{1,0:...) custom-call(s32[2]{0:T(128)} %pad_add_fusion.place_ref, ...), custom_call_target="tpu_custom_call" | custom-call | tf_op jit(solution)/shard_map/layer_forward/pallas_call | solution.py:382
  212.3 3.6 collective-permute-start.48
  217.9 3.7 collective-permute-done.47
  222.3 30.3 %layer_backward.2 = (bf16[1024,384]{1,0:T(8,128)(2,1)}, bf16[1024,384]{1,0:T(8,128)(2,1)}, bf16[1024,384]{1,0:T(8,128)(2,1)}, bf16[256,1024]{1,0:T(8,128)(2,1)},...) custom-call(s32[2]{0:T(128)} %pad_add_fusion.place_ref, ...), custom_call_target="tpu_custom_call" | custom-call | tf_op jit(solution)/shard_map/layer_backward/pallas_call | solution.py:382
  257.1 4.1 fold.6
  268.9 13.5 %collective-permute-done.50.a_ref = bf16[128,1536]{1,0:T(8,128)(2,1)S(1)} collective-permute-done((bf16[128,1536]{1,0:T(8,128)(2,1)}, bf16[128,1536]{1,0:T(8,128)(2,1)S(1)}, u32[]{:S(2)}, u32[]{:S(2)}) %collective-permute-start.50) | collective-permute-done | bytes 393248 | tf_op jit(solution)/shard_map/ppermute | solution.py:522
  284.9 4.0 convolution_convert_fusion.2
  288.9 3.8 between_layers.1
  302.0 8.4 %collective-permute-start.102 = (bf16[1536,384]{1,0:T(8,128)(2,1)}, bf16[1536,384]{1,0:T(8,128)(2,1)}, u32[]{:S(2)}, u32[]{:S(2)}) collective-permute-start(bf16[1536,384]{1,0:T(8,128)(2,1)} %convolution_convert_fusion.1), channel_id=1, source_target_pairs={{0,8},{1,9},{2,10},{3,11},{12,4},{13,5},{14,6},{15,7},{16,24},{17,... | collective-permute-start | bytes 3538952 | tf_op jit(solution)/shard_map/ppermute | solution.py:522
  318.9 4.3 fold.5
  337.5 13.0 %collective-permute-start.53 = (bf16[128,1664]{1,0:T(8,128)(2,1)S(1)}, bf16[128,1664]{1,0:T(8,128)(2,1)S(1)}, u32[]{:S(2)}, u32[]{:S(2)}) collective-permute-start(bf16[128,1664]{1,0:T(8,128)(2,1)S(1)} %copy-done.40), channel_id=1, source_target_pairs={{0,8},{1,9},{2,10},{3,11},{4,12},{5,13},{6,14},{7,15},{8,0},{9,1},... | collective-permute-start | bytes 1277960 | tf_op jit(solution)/shard_map/ppermute | solution.py:522
  353.8 3.3 add_convert_fusion
  360.1 7.6 %collective-permute-start.44 = (f32[128,1536]{1,0:T(8,128)}, f32[128,1536]{1,0:T(8,128)}, u32[]{:S(2)}, u32[]{:S(2)}) collective-permute-start(f32[128,1536]{1,0:T(8,128)} %last_output.1), channel_id=1, source_target_pairs={{0,0},{1,1},{2,2},{3,3},{4,8},{5,9},{6,10},{7,11},{8,4},{9,5},{10,... | collective-permute-start | bytes 2359304 | tf_op jit(solution)/shard_map/ppermute | solution.py:522
  369.5 4.6 assemble.7.refs_0_
  374.6 31.5 %layer_backward.3 = (bf16[1024,384]{1,0:T(8,128)(2,1)}, bf16[1024,384]{1,0:T(8,128)(2,1)}, bf16[1024,384]{1,0:T(8,128)(2,1)}, bf16[256,1024]{1,0:T(8,128)(2,1)},...) custom-call(s32[2]{0:T(128)} %pad_add_fusion.place_ref, ...), custom_call_target="tpu_custom_call" | custom-call | tf_op jit(solution)/shard_map/layer_backward/pallas_call | solution.py:382
  429.0 3.3 collective-permute-done.70
  435.8 3.9 concatenate.56
  440.5 5.4 collective-permute-start.80
  451.3 8.8 %collective-permute-done.81 = bf16[64,1536]{1,0:T(8,128)(2,1)S(1)} collective-permute-done((bf16[64,1536]{1,0:T(8,128)(2,1)}, bf16[64,1536]{1,0:T(8,128)(2,1)S(1)}, u32[]{:S(2)}, u32[]{:S(2)}) %collective-permute-start.81) | collective-permute-done | bytes 196640 | tf_op jit(solution)/shard_map/ppermute | solution.py:522
  476.2 8.0 %collective-permute-start.91 = (bf16[1536,384]{1,0:T(8,128)(2,1)}, bf16[1536,384]{1,0:T(8,128)(2,1)}, u32[]{:S(2)}, u32[]{:S(2)}) collective-permute-start(bf16[1536,384]{1,0:T(8,128)(2,1)} %convolution_convert_fusion.3), channel_id=1, source_target_pairs={{0,8},{1,9},{2,10},{3,11},{12,4},{13,5},{14,6},{15,7},{16,24},{17,... | collective-permute-start | bytes 3538952 | tf_op jit(solution)/shard_map/ppermute | solution.py:522
  494.7 5.5 collective-permute-done.88
  500.4 4.1 collective-permute-done.89
  507.2 5.4 collective-permute-start.62
  513.9 5.0 collective-permute-start.90
  536.4 4.7 collective-permute-done.113
  550.3 9.7 %collective-permute-done.96 = bf16[384,384]{1,0:T(8,128)(2,1)S(1)} collective-permute-done((bf16[384,384]{1,0:T(8,128)(2,1)S(1)}, bf16[384,384]{1,0:T(8,128)(2,1)S(1)}, u32[]{:S(2)}, u32[]{:S(2)}) %collective-permute-start.96) | collective-permute-done | bytes 294944 | tf_op jit(solution)/shard_map/ppermute | solution.py:522
  560.1 7.4 %collective-permute-start.67 = (f32[128,1536]{1,0:T(8,128)}, f32[128,1536]{1,0:T(8,128)}, u32[]{:S(2)}, u32[]{:S(2)}) collective-permute-start(f32[128,1536]{1,0:T(8,128)} %get-tuple-element.143), channel_id=1, source_target_pairs={{0,0},{1,1},{2,2},{3,3},{4,8},{5,9},{6,10},{7,11},{8,4},{9,5},{10,... | collective-permute-start | bytes 2359304 | tf_op jit(solution)/shard_map/ppermute | solution.py:522
  567.5 3.7 collective-permute-start.115
  574.0 5.1 collective-permute-done.97
  585.1 4.0 fold.7
  592.4 4.8 collective-permute-done.99
  610.5 4.2 collective-permute-done.64.a_ref
  614.8 5.4 collective-permute-done.65.b_ref
  623.4 3.2 input_gradient.1
  628.1 4.3 fusion.38
  (555 shorter events, 246.6 us)
Async XLA Ops:
  7.2 477.0 %all-reduce.13.cloned.1.call-start = ((), (), s32[]{:S(2)}) async-start(), calls=%async_computation | async-start | bytes 3538944 | tf_op jit(solution)/shard_map/psum | solution.py:702
  11.7 37.0 %collective-permute-start.13 = (f32[16,512]{1,0:T(8,128)}, f32[16,512]{1,0:T(8,128)}, u32[]{:S(2)}, u32[]{:S(2)}) collective-permute-start(f32[16,512]{1,0:T(8,128)} %fusion.23), channel_id=1, source_target_pairs={{0,0},{1,1},{2,2},{3,3},{4,8},{5,9},{6,10},{7,11},{8,4},{9,5},{10,... | collective-permute-start | bytes 98312 | tf_op jit(solution)/shard_map/ppermute | solution.py:522
  20.8 21.5 %collective-permute-start.11 = (bf16[1536,384]{1,0:T(8,128)(2,1)}, bf16[1536,384]{1,0:T(8,128)(2,1)S(1)}, u32[]{:S(2)}, u32[]{:S(2)}) collective-permute-start(bf16[1536,384]{1,0:T(8,128)(2,1)} %get-tuple-element.91), channel_id=1, source_target_pairs={{0,0},{1,1},{2,2},{3,3},{4,8},{5,9},{6,10},{7,11},{8,4},{9,5},{10,... | collective-permute-start | bytes 3538952 | tf_op jit(solution)/shard_map/ppermute | solution.py:522
  25.5 18.9 %collective-permute-start.2 = (bf16[160,1536]{1,0:T(8,128)(2,1)}, bf16[160,1536]{1,0:T(8,128)(2,1)S(1)}, u32[]{:S(2)}, u32[]{:S(2)}) collective-permute-start(bf16[160,1536]{1,0:T(8,128)(2,1)} %first_norm.1.refs_0_), channel_id=1, source_target_pairs={{0,1},{1,2},{2,3},{3,0},{4,5},{5,6},{6,7},{7,4},{8,9},{9,10},{10,1... | collective-permute-start | bytes 1474568 | tf_op jit(solution)/shard_map/ppermute | solution.py:522
  27.4 19.0 %collective-permute-start.4 = (bf16[160,1536]{1,0:T(8,128)(2,1)}, bf16[160,1536]{1,0:T(8,128)(2,1)S(1)}, u32[]{:S(2)}, u32[]{:S(2)}) collective-permute-start(bf16[160,1536]{1,0:T(8,128)(2,1)} %first_norm.1.refs_0_), channel_id=1, source_target_pairs={{0,3},{1,0},{2,1},{3,2},{4,7},{5,4},{6,5},{7,6},{8,11},{9,8},{10,9... | collective-permute-start | bytes 1474568 | tf_op jit(solution)/shard_map/ppermute | solution.py:522
  29.6 36.5 %collective-permute-start.1 = (bf16[160,1536]{1,0:T(8,128)(2,1)}, bf16[160,1536]{1,0:T(8,128)(2,1)S(1)}, u32[]{:S(2)}, u32[]{:S(2)}) collective-permute-start(bf16[160,1536]{1,0:T(8,128)(2,1)} %first_norm.1.refs_0_), channel_id=1, source_target_pairs={{0,8},{1,9},{2,10},{3,11},{4,12},{5,13},{6,14},{7,15},{8,0},{9,1},... | collective-permute-start | bytes 1474568 | tf_op jit(solution)/shard_map/ppermute | solution.py:522
  42.3 34.0 %collective-permute-start.12 = (bf16[384,1536]{1,0:T(8,128)(2,1)S(1)}, bf16[384,1536]{1,0:T(8,128)(2,1)S(1)}, u32[]{:S(2)}, u32[]{:S(2)}) collective-permute-start(bf16[384,1536]{1,0:T(8,128)(2,1)S(1)} %get-tuple-element.93), channel_id=1, source_target_pairs={{0,0},{1,1},{2,2},{3,3},{4,8},{5,9},{6,10},{7,11},{8,4},{9,5},{10,... | collective-permute-start | bytes 3538952 | tf_op jit(solution)/shard_map/ppermute | solution.py:522
  44.4 23.1 %collective-permute-start.6 = (bf16[80,1536]{1,0:T(8,128)(2,1)S(1)}, bf16[80,1536]{1,0:T(8,128)(2,1)S(1)}, u32[]{:S(2)}, u32[]{:S(2)}) collective-permute-start(bf16[80,1536]{1,0:T(8,128)(2,1)S(1)} %slice.284), channel_id=1, source_target_pairs={{0,1},{1,2},{2,3},{3,0},{4,5},{5,6},{6,7},{7,4},{8,9},{9,10},{10,1... | collective-permute-start | bytes 737288 | tf_op jit(solution)/shard_map/ppermute | solution.py:522
  46.4 21.8 %collective-permute-start.8 = (bf16[80,1536]{1,0:T(8,128)(2,1)S(1)}, bf16[80,1536]{1,0:T(8,128)(2,1)S(1)}, u32[]{:S(2)}, u32[]{:S(2)}) collective-permute-start(bf16[80,1536]{1,0:T(8,128)(2,1)S(1)} %slice.285), channel_id=1, source_target_pairs={{0,3},{1,0},{2,1},{3,2},{4,7},{5,4},{6,5},{7,6},{8,11},{9,8},{10,9... | collective-permute-start | bytes 737288 | tf_op jit(solution)/shard_map/ppermute | solution.py:522
  50.0 19.9 %collective-permute-start.3 = (bf16[160,1536]{1,0:T(8,128)(2,1)S(1)}, bf16[160,1536]{1,0:T(8,128)(2,1)S(1)}, u32[]{:S(2)}, u32[]{:S(2)}) collective-permute-start(bf16[160,1536]{1,0:T(8,128)(2,1)S(1)} %collective-permute-done.2.refs_2_), channel_id=1, source_target_pairs={{0,8},{1,9},{2,10},{3,11},{4,12},{5,13},{6,14},{7,15},{8,0},{9,1},... | collective-permute-start | bytes 1474568 | tf_op jit(solution)/shard_map/ppermute | solution.py:522
  100.2 36.0 %collective-permute-start.28 = (bf16[1536,384]{1,0:T(8,128)(2,1)S(1)}, bf16[1536,384]{1,0:T(8,128)(2,1)S(1)}, u32[]{:S(2)}, u32[]{:S(2)}) collective-permute-start(bf16[1536,384]{1,0:T(8,128)(2,1)S(1)} %copy-done.20), channel_id=1, source_target_pairs={{0,0},{1,1},{2,2},{3,3},{4,8},{5,9},{6,10},{7,11},{8,4},{9,5},{10,... | collective-permute-start | bytes 3538952 | tf_op jit(solution)/shard_map/ppermute | solution.py:522
  109.6 27.7 %collective-permute-start.15 = (bf16[128,1664]{1,0:T(8,128)(2,1)}, bf16[128,1664]{1,0:T(8,128)(2,1)S(1)}, u32[]{:S(2)}, u32[]{:S(2)}) collective-permute-start(bf16[128,1664]{1,0:T(8,128)(2,1)} %get-tuple-element.97), channel_id=1, source_target_pairs={{0,1},{1,2},{2,3},{3,0},{4,5},{5,6},{6,7},{7,4},{8,9},{9,10},{10,1... | collective-permute-start | bytes 1277960 | tf_op jit(solution)/shard_map/ppermute | solution.py:522
  111.2 28.8 %collective-permute-start.16 = (bf16[128,1664]{1,0:T(8,128)(2,1)}, bf16[128,1664]{1,0:T(8,128)(2,1)S(1)}, u32[]{:S(2)}, u32[]{:S(2)}) collective-permute-start(bf16[128,1664]{1,0:T(8,128)(2,1)} %get-tuple-element.98), channel_id=1, source_target_pairs={{0,2},{1,3},{2,0},{3,1},{4,6},{5,7},{6,4},{7,5},{8,10},{9,11},{10,... | collective-permute-start | bytes 1277960 | tf_op jit(solution)/shard_map/ppermute | solution.py:522
  112.7 28.9 %collective-permute-start.17 = (bf16[128,1664]{1,0:T(8,128)(2,1)}, bf16[128,1664]{1,0:T(8,128)(2,1)}, u32[]{:S(2)}, u32[]{:S(2)}) collective-permute-start(bf16[128,1664]{1,0:T(8,128)(2,1)} %get-tuple-element.99), channel_id=1, source_target_pairs={{0,3},{1,0},{2,1},{3,2},{4,7},{5,4},{6,5},{7,6},{8,11},{9,8},{10,9... | collective-permute-start | bytes 1277960 | tf_op jit(solution)/shard_map/ppermute | solution.py:522
  114.4 31.2 %collective-permute-start.30 = (bf16[160,1536]{1,0:T(8,128)(2,1)S(1)}, bf16[160,1536]{1,0:T(8,128)(2,1)S(1)}, u32[]{:S(2)}, u32[]{:S(2)}) collective-permute-start(bf16[160,1536]{1,0:T(8,128)(2,1)S(1)} %collective-permute-done.29.refs_0_.dres_ref), channel_id=1, source_target_pairs={{0,8},{1,9},{2,10},{3,11},{4,12},{5,13},{6,14},{7,15},{8,0},{9,1},... | collective-permute-start | bytes 1474568 | tf_op jit(solution)/shard_map/ppermute | solution.py:522
  137.3 23.1 %collective-permute-start.32 = (bf16[160,1536]{1,0:T(8,128)(2,1)}, bf16[160,1536]{1,0:T(8,128)(2,1)S(1)}, u32[]{:S(2)}, u32[]{:S(2)}) collective-permute-start(bf16[160,1536]{1,0:T(8,128)(2,1)} %collective-permute-done.31.refs_2_), channel_id=1, source_target_pairs={{0,8},{1,9},{2,10},{3,11},{4,12},{5,13},{6,14},{7,15},{8,0},{9,1},... | collective-permute-start | bytes 1474568 | tf_op jit(solution)/shard_map/ppermute | solution.py:522
  139.9 45.8 %collective-permute-start.39 = (bf16[384,1536]{1,0:T(8,128)(2,1)S(1)}, bf16[384,1536]{1,0:T(8,128)(2,1)S(1)}, u32[]{:S(2)}, u32[]{:S(2)}) collective-permute-start(bf16[384,1536]{1,0:T(8,128)(2,1)S(1)} %get-tuple-element.105), channel_id=1, source_target_pairs={{0,0},{1,1},{2,2},{3,3},{4,8},{5,9},{6,10},{7,11},{8,4},{9,5},{10,... | collective-permute-start | bytes 3538952 | tf_op jit(solution)/shard_map/ppermute | solution.py:522
  252.9 49.1 %collective-permute-start.40 = (bf16[512,1664]{1,0:T(8,128)(2,1)}, bf16[512,1664]{1,0:T(8,128)(2,1)}, u32[]{:S(2)}, u32[]{:S(2)}) collective-permute-start(bf16[512,1664]{1,0:T(8,128)(2,1)} %get-tuple-element.108), channel_id=1, source_target_pairs={{0,8},{1,9},{2,10},{3,11},{4,12},{5,13},{6,14},{7,15},{8,0},{9,1},... | collective-permute-start | bytes 5111816 | tf_op jit(solution)/shard_map/ppermute | solution.py:522
  261.1 21.2 %collective-permute-start.50 = (bf16[128,1536]{1,0:T(8,128)(2,1)}, bf16[128,1536]{1,0:T(8,128)(2,1)S(1)}, u32[]{:S(2)}, u32[]{:S(2)}) collective-permute-start(bf16[128,1536]{1,0:T(8,128)(2,1)} %get-tuple-element.125), channel_id=1, source_target_pairs={{0,1},{1,2},{2,3},{3,0},{4,5},{5,6},{6,7},{7,4},{8,9},{9,10},{10,1... | collective-permute-start | bytes 1179656 | tf_op jit(solution)/shard_map/ppermute | solution.py:522
  261.2 21.2 %collective-permute-start.51 = (bf16[128,1536]{1,0:T(8,128)(2,1)}, bf16[128,1536]{1,0:T(8,128)(2,1)S(1)}, u32[]{:S(2)}, u32[]{:S(2)}) collective-permute-start(bf16[128,1536]{1,0:T(8,128)(2,1)} %get-tuple-element.126), channel_id=1, source_target_pairs={{0,2},{1,3},{2,0},{3,1},{4,6},{5,7},{6,4},{7,5},{8,10},{9,11},{10,... | collective-permute-start | bytes 1179656 | tf_op jit(solution)/shard_map/ppermute | solution.py:522
  263.4 19.7 %collective-permute-start.52 = (bf16[128,1536]{1,0:T(8,128)(2,1)}, bf16[128,1536]{1,0:T(8,128)(2,1)S(1)}, u32[]{:S(2)}, u32[]{:S(2)}) collective-permute-start(bf16[128,1536]{1,0:T(8,128)(2,1)} %get-tuple-element.127), channel_id=1, source_target_pairs={{0,3},{1,0},{2,1},{3,2},{4,7},{5,4},{6,5},{7,6},{8,11},{9,8},{10,9... | collective-permute-start | bytes 1179656 | tf_op jit(solution)/shard_map/ppermute | solution.py:522
  266.6 33.7 %collective-permute-start.118 = (bf16[192,1536]{1,0:T(8,128)(2,1)S(1)}, bf16[192,1536]{1,0:T(8,128)(2,1)}, u32[]{:S(2)}, u32[]{:S(2)}) collective-permute-start(bf16[192,1536]{1,0:T(8,128)(2,1)S(1)} %get-tuple-element.228), channel_id=1, source_target_pairs={{4,0},{5,1},{6,2},{7,3},{8,12},{9,13},{10,14},{11,15},{20,16},{21,... | collective-permute-start | bytes 1769480 | tf_op jit(solution)/shard_map/ppermute | solution.py:522
  292.7 35.3 %collective-permute-start.103 = (bf16[1536,384]{1,0:T(8,128)(2,1)}, bf16[1536,384]{1,0:T(8,128)(2,1)}, u32[]{:S(2)}, u32[]{:S(2)}) collective-permute-start(bf16[1536,384]{1,0:T(8,128)(2,1)} %convolution_convert_fusion.2), channel_id=1, source_target_pairs={{4,0},{5,1},{6,2},{7,3},{8,12},{9,13},{10,14},{11,15},{20,16},{21,... | collective-permute-start | bytes 3538952 | tf_op jit(solution)/shard_map/ppermute | solution.py:522
  300.2 30.4 %collective-permute-start.104 = (bf16[1536,384]{1,0:T(8,128)(2,1)}, bf16[1536,384]{1,0:T(8,128)(2,1)}, u32[]{:S(2)}, u32[]{:S(2)}) collective-permute-start(bf16[1536,384]{1,0:T(8,128)(2,1)} %convolution_convert_fusion.1), channel_id=1, source_target_pairs={{4,8},{5,9},{6,10},{7,11},{8,4},{9,5},{10,6},{11,7},{20,24},{21,25... | collective-permute-start | bytes 3538952 | tf_op jit(solution)/shard_map/ppermute | solution.py:522
  302.0 28.6 %collective-permute-start.102 = (bf16[1536,384]{1,0:T(8,128)(2,1)}, bf16[1536,384]{1,0:T(8,128)(2,1)}, u32[]{:S(2)}, u32[]{:S(2)}) collective-permute-start(bf16[1536,384]{1,0:T(8,128)(2,1)} %convolution_convert_fusion.1), channel_id=1, source_target_pairs={{0,8},{1,9},{2,10},{3,11},{12,4},{13,5},{14,6},{15,7},{16,24},{17,... | collective-permute-start | bytes 3538952 | tf_op jit(solution)/shard_map/ppermute | solution.py:522
  325.9 24.6 %collective-permute-start.42 = (bf16[128,1664]{1,0:T(8,128)(2,1)}, bf16[128,1664]{1,0:T(8,128)(2,1)S(1)}, u32[]{:S(2)}, u32[]{:S(2)}) collective-permute-start(bf16[128,1664]{1,0:T(8,128)(2,1)} %get-tuple-element.111), channel_id=1, source_target_pairs={{0,2},{1,3},{2,0},{3,1},{4,6},{5,7},{6,4},{7,5},{8,10},{9,11},{10,... | collective-permute-start | bytes 1277960 | tf_op jit(solution)/shard_map/ppermute | solution.py:522
  328.1 22.5 %collective-permute-start.43 = (bf16[128,1664]{1,0:T(8,128)(2,1)}, bf16[128,1664]{1,0:T(8,128)(2,1)S(1)}, u32[]{:S(2)}, u32[]{:S(2)}) collective-permute-start(bf16[128,1664]{1,0:T(8,128)(2,1)} %get-tuple-element.112), channel_id=1, source_target_pairs={{0,3},{1,0},{2,1},{3,2},{4,7},{5,4},{6,5},{7,6},{8,11},{9,8},{10,9... | collective-permute-start | bytes 1277960 | tf_op jit(solution)/shard_map/ppermute | solution.py:522
  330.6 20.8 %collective-permute-start.58 = (bf16[64,1664]{1,0:T(8,128)(2,1)S(1)}, bf16[64,1664]{1,0:T(8,128)(2,1)}, u32[]{:S(2)}, u32[]{:S(2)}) collective-permute-start(bf16[64,1664]{1,0:T(8,128)(2,1)S(1)} %slice.297), channel_id=1, source_target_pairs={{0,1},{1,2},{2,3},{3,0},{4,5},{5,6},{6,7},{7,4},{8,9},{9,10},{10,1... | collective-permute-start | bytes 638984 | tf_op jit(solution)/shard_map/ppermute | solution.py:522
  330.6 22.3 %collective-permute-start.60 = (bf16[64,1664]{1,0:T(8,128)(2,1)S(1)}, bf16[64,1664]{1,0:T(8,128)(2,1)}, u32[]{:S(2)}, u32[]{:S(2)}) collective-permute-start(bf16[64,1664]{1,0:T(8,128)(2,1)S(1)} %slice.298), channel_id=1, source_target_pairs={{0,3},{1,0},{2,1},{3,2},{4,7},{5,4},{6,5},{7,6},{8,11},{9,8},{10,9... | collective-permute-start | bytes 638984 | tf_op jit(solution)/shard_map/ppermute | solution.py:522
  337.5 22.6 %collective-permute-start.53 = (bf16[128,1664]{1,0:T(8,128)(2,1)S(1)}, bf16[128,1664]{1,0:T(8,128)(2,1)S(1)}, u32[]{:S(2)}, u32[]{:S(2)}) collective-permute-start(bf16[128,1664]{1,0:T(8,128)(2,1)S(1)} %copy-done.40), channel_id=1, source_target_pairs={{0,8},{1,9},{2,10},{3,11},{4,12},{5,13},{6,14},{7,15},{8,0},{9,1},... | collective-permute-start | bytes 1277960 | tf_op jit(solution)/shard_map/ppermute | solution.py:522
  360.1 108.6 %collective-permute-start.44 = (f32[128,1536]{1,0:T(8,128)}, f32[128,1536]{1,0:T(8,128)}, u32[]{:S(2)}, u32[]{:S(2)}) collective-permute-start(f32[128,1536]{1,0:T(8,128)} %last_output.1), channel_id=1, source_target_pairs={{0,0},{1,1},{2,2},{3,3},{4,8},{5,9},{6,10},{7,11},{8,4},{9,5},{10,... | collective-permute-start | bytes 2359304 | tf_op jit(solution)/shard_map/ppermute | solution.py:522
  439.7 22.6 %collective-permute-start.82 = (bf16[64,1536]{1,0:T(8,128)(2,1)S(1)}, bf16[64,1536]{1,0:T(8,128)(2,1)S(1)}, u32[]{:S(2)}, u32[]{:S(2)}) collective-permute-start(bf16[64,1536]{1,0:T(8,128)(2,1)S(1)} %pad_slice_fusion), channel_id=1, source_target_pairs={{4,8},{5,9},{6,10},{7,11},{8,4},{9,5},{10,6},{11,7},{20,24},{21,25... | collective-permute-start | bytes 589832 | tf_op jit(solution)/shard_map/ppermute | solution.py:522
  440.5 21.7 %collective-permute-start.80 = (bf16[64,1536]{1,0:T(8,128)(2,1)S(1)}, bf16[64,1536]{1,0:T(8,128)(2,1)S(1)}, u32[]{:S(2)}, u32[]{:S(2)}) collective-permute-start(bf16[64,1536]{1,0:T(8,128)(2,1)S(1)} %pad_slice_fusion), channel_id=1, source_target_pairs={{0,8},{1,9},{2,10},{3,11},{12,4},{13,5},{14,6},{15,7},{16,24},{17,... | collective-permute-start | bytes 589832 | tf_op jit(solution)/shard_map/ppermute | solution.py:522
  449.5 34.9 %collective-permute-start.108 = (bf16[192,1536]{1,0:T(8,128)(2,1)}, bf16[192,1536]{1,0:T(8,128)(2,1)}, u32[]{:S(2)}, u32[]{:S(2)}) collective-permute-start(bf16[192,1536]{1,0:T(8,128)(2,1)} %get-tuple-element.220), channel_id=1, source_target_pairs={{4,8},{5,9},{6,10},{7,11},{8,4},{9,5},{10,6},{11,7},{20,24},{21,25... | collective-permute-start | bytes 1769480 | tf_op jit(solution)/shard_map/ppermute | solution.py:522
  460.1 25.8 %collective-permute-start.106 = (bf16[192,1536]{1,0:T(8,128)(2,1)}, bf16[192,1536]{1,0:T(8,128)(2,1)}, u32[]{:S(2)}, u32[]{:S(2)}) collective-permute-start(bf16[192,1536]{1,0:T(8,128)(2,1)} %get-tuple-element.220), channel_id=1, source_target_pairs={{0,8},{1,9},{2,10},{3,11},{12,4},{13,5},{14,6},{15,7},{16,24},{17,... | collective-permute-start | bytes 1769480 | tf_op jit(solution)/shard_map/ppermute | solution.py:522
  474.4 68.4 %collective-permute-start.93 = (bf16[1536,384]{1,0:T(8,128)(2,1)}, bf16[1536,384]{1,0:T(8,128)(2,1)}, u32[]{:S(2)}, u32[]{:S(2)}) collective-permute-start(bf16[1536,384]{1,0:T(8,128)(2,1)} %convolution_convert_fusion.3), channel_id=1, source_target_pairs={{4,8},{5,9},{6,10},{7,11},{8,4},{9,5},{10,6},{11,7},{20,24},{21,25... | collective-permute-start | bytes 3538952 | tf_op jit(solution)/shard_map/ppermute | solution.py:522
  476.2 66.7 %collective-permute-start.91 = (bf16[1536,384]{1,0:T(8,128)(2,1)}, bf16[1536,384]{1,0:T(8,128)(2,1)}, u32[]{:S(2)}, u32[]{:S(2)}) collective-permute-start(bf16[1536,384]{1,0:T(8,128)(2,1)} %convolution_convert_fusion.3), channel_id=1, source_target_pairs={{0,8},{1,9},{2,10},{3,11},{12,4},{13,5},{14,6},{15,7},{16,24},{17,... | collective-permute-start | bytes 3538952 | tf_op jit(solution)/shard_map/ppermute | solution.py:522
  484.3 20.6 %collective-permute-start.120 = (bf16[192,1536]{1,0:T(8,128)(2,1)}, bf16[192,1536]{1,0:T(8,128)(2,1)S(1)}, u32[]{:S(2)}, u32[]{:S(2)}) collective-permute-start(bf16[192,1536]{1,0:T(8,128)(2,1)} %get-tuple-element.195), channel_id=1, source_target_pairs={{0,8},{1,9},{2,10},{3,11},{4,12},{5,13},{6,14},{7,15},{8,0},{9,1},... | collective-permute-start | bytes 1769480 | tf_op jit(solution)/shard_map/ppermute | solution.py:522
  507.2 76.7 %collective-permute-start.62 = (bf16[512,1536]{1,0:T(8,128)(2,1)}, bf16[512,1536]{1,0:T(8,128)(2,1)S(1)}, u32[]{:S(2)}, u32[]{:S(2)}) collective-permute-start(bf16[512,1536]{1,0:T(8,128)(2,1)} %get-tuple-element.138), channel_id=1, source_target_pairs={{0,8},{1,9},{2,10},{3,11},{4,12},{5,13},{6,14},{7,15},{8,0},{9,1},... | collective-permute-start | bytes 4718600 | tf_op jit(solution)/shard_map/ppermute | solution.py:522
  512.6 30.0 %collective-permute-start.92 = (bf16[1536,384]{1,0:T(8,128)(2,1)}, bf16[1536,384]{1,0:T(8,128)(2,1)}, u32[]{:S(2)}, u32[]{:S(2)}) collective-permute-start(bf16[1536,384]{1,0:T(8,128)(2,1)} %convolution_convert_fusion.4), channel_id=1, source_target_pairs={{4,0},{5,1},{6,2},{7,3},{8,12},{9,13},{10,14},{11,15},{20,16},{21,... | collective-permute-start | bytes 3538952 | tf_op jit(solution)/shard_map/ppermute | solution.py:522
  541.1 39.6 %collective-permute-start.105 = (bf16[1536,384]{1,0:T(8,128)(2,1)S(1)}, bf16[1536,384]{1,0:T(8,128)(2,1)S(1)}, u32[]{:S(2)}, u32[]{:S(2)}) collective-permute-start(bf16[1536,384]{1,0:T(8,128)(2,1)S(1)} %copy-done.18), channel_id=1, source_target_pairs={{0,8},{1,9},{2,10},{3,11},{4,12},{5,13},{6,14},{7,15},{8,0},{9,1},... | collective-permute-start | bytes 3538952 | tf_op jit(solution)/shard_map/ppermute | solution.py:522
  547.6 19.9 %collective-permute-start.95 = (bf16[384,384]{1,0:T(8,128)(2,1)S(1)}, bf16[384,384]{1,0:T(8,128)(2,1)S(1)}, u32[]{:S(2)}, u32[]{:S(2)}) collective-permute-start(bf16[384,384]{1,0:T(8,128)(2,1)S(1)} %get-tuple-element.226), channel_id=1, source_target_pairs={{0,64},{1,65},{2,66},{3,67},{4,68},{5,69},{6,70},{7,71},{8,72},{9,... | collective-permute-start | bytes 884744 | tf_op jit(solution)/shard_map/ppermute | solution.py:522
  550.0 21.2 %collective-permute-start.94 = (bf16[384,384]{1,0:T(8,128)(2,1)S(1)}, bf16[384,384]{1,0:T(8,128)(2,1)S(1)}, u32[]{:S(2)}, u32[]{:S(2)}) collective-permute-start(bf16[384,384]{1,0:T(8,128)(2,1)S(1)} %get-tuple-element.224), channel_id=1, source_target_pairs={{0,32},{1,33},{2,34},{3,35},{4,36},{5,37},{6,38},{7,39},{8,40},{9,... | collective-permute-start | bytes 884744 | tf_op jit(solution)/shard_map/ppermute | solution.py:522
  560.1 46.6 %collective-permute-start.67 = (f32[128,1536]{1,0:T(8,128)}, f32[128,1536]{1,0:T(8,128)}, u32[]{:S(2)}, u32[]{:S(2)}) collective-permute-start(f32[128,1536]{1,0:T(8,128)} %get-tuple-element.143), channel_id=1, source_target_pairs={{0,0},{1,1},{2,2},{3,3},{4,8},{5,9},{6,10},{7,11},{8,4},{9,5},{10,... | collective-permute-start | bytes 2359304 | tf_op jit(solution)/shard_map/ppermute | solution.py:522
  573.9 29.7 %collective-permute-start.116 = (bf16[192,1536]{1,0:T(8,128)(2,1)S(1)}, bf16[192,1536]{1,0:T(8,128)(2,1)S(1)}, u32[]{:S(2)}, u32[]{:S(2)}) collective-permute-start(bf16[192,1536]{1,0:T(8,128)(2,1)S(1)} %bitcast.233), channel_id=1, source_target_pairs={{0,8},{1,9},{2,10},{3,11},{4,12},{5,13},{6,14},{7,15},{8,0},{9,1},... | collective-permute-start | bytes 1769480 | tf_op jit(solution)/shard_map/ppermute | solution.py:522
  589.0 21.5 %collective-permute-start.63 = (bf16[128,1536]{1,0:T(8,128)(2,1)}, bf16[128,1536]{1,0:T(8,128)(2,1)S(1)}, u32[]{:S(2)}, u32[]{:S(2)}) collective-permute-start(bf16[128,1536]{1,0:T(8,128)(2,1)} %get-tuple-element.139), channel_id=1, source_target_pairs={{0,0},{1,1},{2,2},{3,3},{4,8},{5,9},{6,10},{7,11},{8,4},{9,5},{10,... | collective-permute-start | bytes 1179656 | tf_op jit(solution)/shard_map/ppermute | solution.py:522
  600.4 19.8 %collective-permute-start.65 = (bf16[128,1536]{1,0:T(8,128)(2,1)S(1)}, bf16[128,1536]{1,0:T(8,128)(2,1)S(1)}, u32[]{:S(2)}, u32[]{:S(2)}) collective-permute-start(bf16[128,1536]{1,0:T(8,128)(2,1)S(1)} %copy-done.97), channel_id=1, source_target_pairs={{0,2},{1,3},{2,0},{3,1},{4,10},{5,11},{6,8},{7,9},{8,6},{9,7},{10,... | collective-permute-start | bytes 1179656 | tf_op jit(solution)/shard_map/ppermute | solution.py:522
  604.4 22.2 %collective-permute-start.101 = (bf16[1536,384]{1,0:T(8,128)(2,1)S(1)}, bf16[1536,384]{1,0:T(8,128)(2,1)S(1)}, u32[]{:S(2)}, u32[]{:S(2)}) collective-permute-start(bf16[1536,384]{1,0:T(8,128)(2,1)S(1)} %bitcast.230), channel_id=1, source_target_pairs={{0,8},{1,9},{2,10},{3,11},{4,12},{5,13},{6,14},{7,15},{8,0},{9,1},... | collective-permute-start | bytes 3538952 | tf_op jit(solution)/shard_map/ppermute | solution.py:522
  (172 other events, 1646.1 us)
Sparse Core Ops, SparseCore 0:
  357.2 100.8 all-reduce.12
